TPU v7x, 256 devices: a whole 4x4x8 slice. The times are simulated.
256 devices in a mesh: scene: 4 (over x), tile: 64 (over y, z, core).
Axes of the slice: x: 4, y: 4, z: 8, core: 2. Of those that a mesh axis runs over, the one named last changes fastest.
Arguments:
- blocks: bfloat16 [4, 128, 128, 512], P('scene', 'tile'), may hold values from -6 to 6
- block_position: int32 [4, 128], P('scene', 'tile'), may hold values from 0 to 15, as said below
- block_frame: int32 [4, 128], P('scene', 'tile'), may hold values from 0 to 7
- block_count: int32 [4, 64], P('scene', 'tile'), may hold values from 1 to 2, as said below
- weights: bfloat16 [8, 512, 512], replicated, may hold values from -0.25 to 0.25
- cotangent: bfloat16 [4, 16, 8, 128, 512], P('scene', None, None, 'tile'), may hold values from -6 to 6
Outputs:
- mixed: bfloat16 [4, 16, 8, 128, 512], P('scene', None, None, 'tile')
- input_grad: bfloat16 [4, 128, 128, 512], P('scene', 'tile')
- weight_grad: float32 [2, 2048, 512], P(None, ('scene', 'tile'))
Inputs may be any that keep to these rules, and one draw needn't show every extreme that they name: `block_position`: together with block_frame, each of the 128 pairs of position and frame of a scene is named by exactly one slot of that scene. `block_count`: slots at or past a device's count are ignored; some device of each scene uses all 2.
All inputs are finite; a program needn't handle non-finite values.
Results may differ from a plain program's by a relative error of at most 0.019.
Values may be sent and summed in bfloat16 or wider, within the bound.
A program may use at most 64 MiB of HBM per device.

v0:
```python
import jax
import jax.numpy as jnp
from jax import lax
from jax.sharding import PartitionSpec as P

HEADS = 16
HEAD_DIM = 32


EPSILON = 1e-06


def norm_rows(values):
    return values * lax.rsqrt(jnp.mean(values * values, axis=-1, keepdims=True) + EPSILON)


def right_dot(left_rows, weight):
    return jnp.dot(left_rows, weight, preferred_element_type=jnp.float32)


def right_dot_t(grad_rows, weight):
    return lax.dot_general(
        grad_rows,
        weight,
        (((grad_rows.ndim - 1,), (1,)), ((), ())),
        preferred_element_type=jnp.float32,
    )


def outer_sum(left_rows, grad_rows):
    left_flat = left_rows.reshape(-1, left_rows.shape[-1])
    grad_flat = grad_rows.reshape(-1, grad_rows.shape[-1])
    return lax.dot_general(
        left_flat, grad_flat, (((0,), (0,)), ((), ())), preferred_element_type=jnp.float32
    )


def split_heads(values):
    return values.reshape(values.shape[:-1] + (HEADS, HEAD_DIM))


def block_core(queries, key_rows, values):
    scores = jnp.einsum(
        "bqhe,bkhe->bhqk",
        split_heads(queries),
        split_heads(key_rows),
        preferred_element_type=jnp.float32,
    ) * HEAD_DIM ** (-0.5)
    soft_weights = jax.nn.softmax(scores, axis=-1).astype(jnp.bfloat16)
    context = jnp.einsum(
        "bhqk,bkhe->bqhe", soft_weights, split_heads(values), preferred_element_type=jnp.float32
    )
    return context.astype(jnp.bfloat16).reshape(queries.shape)


def frame_core(queries, key_rows, values, active):
    frame_index = jnp.arange(queries.shape[0])
    allowed = (frame_index[:, None] >= frame_index[None, :]) & active[None, :]
    scores = jnp.einsum(
        "fche,gche->chfg",
        split_heads(queries),
        split_heads(key_rows),
        preferred_element_type=jnp.float32,
    ) * HEAD_DIM ** (-0.5)
    scores = jnp.where(allowed, scores, -1e30)
    soft_weights = jax.nn.softmax(scores, axis=-1).astype(jnp.bfloat16)
    context = jnp.einsum(
        "chfg,gche->fche", soft_weights, split_heads(values), preferred_element_type=jnp.float32
    )
    return context.astype(jnp.bfloat16).reshape(queries.shape)


def piece_forward(inputs, weight_set, core):
    normed = norm_rows(inputs.astype(jnp.float32)).astype(jnp.bfloat16)
    queries = right_dot(normed, weight_set[0]).astype(jnp.bfloat16)
    key_rows = right_dot(normed, weight_set[1]).astype(jnp.bfloat16)
    values = right_dot(normed, weight_set[2]).astype(jnp.bfloat16)
    context, core_back = jax.vjp(core, queries, key_rows, values)
    output = inputs.astype(jnp.float32) + right_dot(context, weight_set[3])
    return (output, (normed, context, core_back))


def piece_backward(inputs, weight_set, saved_parts, grad_out):
    normed, context, core_back = saved_parts
    grad_proj = outer_sum(context, grad_out)
    grad_context = right_dot_t(grad_out, weight_set[3]).astype(jnp.bfloat16)
    grad_query, grad_key, grad_value = core_back(grad_context)
    weight_grads = jnp.stack(
        [
            outer_sum(normed, grad_query),
            outer_sum(normed, grad_key),
            outer_sum(normed, grad_value),
            grad_proj,
        ]
    )
    grad_normed = (
        right_dot_t(grad_query, weight_set[0])
        + right_dot_t(grad_key, weight_set[1])
        + right_dot_t(grad_value, weight_set[2])
    )
    unused, norm_back = jax.vjp(norm_rows, inputs.astype(jnp.float32))
    grad_input = grad_out.astype(jnp.float32) + norm_back(grad_normed)[0]
    return (grad_input, weight_grads)


def place_stack(placing, rows):
    return jnp.einsum("ms,kse->kme", placing, rows, preferred_element_type=jnp.float32).astype(
        jnp.bfloat16
    )


def unplace_stack(placing, rows):
    return jnp.einsum("ms,kme->kse", placing, rows, preferred_element_type=jnp.float32).astype(
        jnp.bfloat16
    )


def body(blocks, block_position, block_frame, block_count, weights, cotangent):
    tile_count = lax.axis_size("tile")
    own_blocks = blocks[0]
    slot_count = own_blocks.shape[0]
    cell_count = own_blocks.shape[1]
    model_width = own_blocks.shape[2]
    position_count = cotangent.shape[1]
    frame_count = cotangent.shape[2]
    cell_share = cotangent.shape[3]
    spatial_w = weights[0:4]
    temporal_w = weights[4:8]
    usable = jnp.arange(slot_count) < block_count[0, 0]
    slot_tag = jnp.where(usable, block_position[0] * frame_count + block_frame[0], -1)
    source_out, spatial_saved = piece_forward(own_blocks, spatial_w, block_core)
    states = source_out.astype(jnp.bfloat16)
    grid_shape = (position_count, frame_count, cell_share, model_width)
    entry_ids = jnp.arange(position_count * frame_count)
    cot_rows = cotangent[0]
    outgoing = states.reshape(slot_count, tile_count, cell_share, model_width)
    tag_rows = jnp.broadcast_to(slot_tag[:, None], (slot_count, tile_count))
    received, tags_in = (
        lax.all_to_all(outgoing, "tile", split_axis=1, concat_axis=1, tiled=True),
        lax.all_to_all(tag_rows, "tile", split_axis=1, concat_axis=1, tiled=True),
    )
    placing_mask = tags_in.reshape(-1)[None, :] == entry_ids[:, None]
    placing = placing_mask.astype(jnp.bfloat16)
    active = jnp.any(placing_mask, axis=1).reshape(position_count, frame_count)
    grid = place_stack(
        placing, received.reshape(1, slot_count * tile_count, cell_share * model_width)
    )[0].reshape(grid_shape)

    def grid_core(queries, key_rows, values):
        return jax.vmap(frame_core)(queries, key_rows, values, active)

    temporal_out, temporal_saved = piece_forward(grid, temporal_w, grid_core)
    keep_mask = active[:, :, None, None]
    mixed_out = jnp.where(keep_mask, temporal_out, 0.0).astype(jnp.bfloat16)
    grad_out = jnp.where(keep_mask, cot_rows, jnp.zeros_like(cot_rows))
    grid_grad32, temporal_grads = piece_backward(grid, temporal_w, temporal_saved, grad_out)
    back_grid = grid_grad32.astype(jnp.bfloat16).reshape(
        1, position_count * frame_count, cell_share * model_width
    )
    sendback = unplace_stack(placing, back_grid)[0].reshape(
        slot_count, tile_count, cell_share, model_width
    )
    returned = lax.all_to_all(sendback, "tile", split_axis=1, concat_axis=1, tiled=True)
    block_grad = returned.reshape(slot_count, cell_count, model_width)
    scaling = (lax.axis_size("scene") * tile_count * slot_count * cell_count) ** (-0.5)
    input_grad32, spatial_grads = piece_backward(own_blocks, spatial_w, spatial_saved, block_grad)
    input_grad = input_grad32.astype(jnp.bfloat16)
    stacked = jnp.stack(
        [
            spatial_grads.reshape(4 * model_width, model_width),
            temporal_grads.reshape(4 * model_width, model_width),
        ]
    )
    grad_total = lax.psum_scatter(stacked, ("scene", "tile"), scatter_dimension=1, tiled=True)
    return (mixed_out[None], input_grad[None], grad_total * scaling)


def solution(mesh):
    return jax.shard_map(
        body,
        mesh=mesh,
        in_specs=(
            P("scene", "tile", None, None),
            P("scene", "tile"),
            P("scene", "tile"),
            P("scene", "tile"),
            P(),
            P("scene", None, None, "tile", None),
        ),
        out_specs=(
            P("scene", None, None, "tile", None),
            P("scene", "tile", None, None),
            P(None, ("scene", "tile"), None),
        ),
        check_vma=False,
    )
```

profile of v0, /device:TPU:32, one launch (start us, length us, event | category | flops | bytes accessed | tf_op | source)
XLA Modules:
  0.0 1441.7 jit_solution(4543120090150028956)
XLA Ops:
  9.1 11.8 all-to-all-start
  20.9 1.1 fusion.45
  22.0 1.1 fusion.47
  23.1 1.4 convolution_convert_fusion.18
  24.5 1.3 convolution_convert_fusion.17
  25.8 1.3 convolution_convert_fusion.19
  27.8 2.2 fusion.114
  30.0 1.9 divide_convert_fusion.1
  32.3 1.4 fusion.21
  35.7 10.3 all-to-all-start.1
  47.9 1.4 convolution_convert_fusion.11
  50.0 7.8 all-to-all-done.1
  58.5 1.2 reshape.320
  59.7 1.3 multiply_reduce_fusion.2
  62.4 2.0 copy.273
  64.4 1.9 fusion.52
  66.3 1.1 copy.274
  68.1 1.3 convolution_convert_fusion.12
  69.5 1.4 convolution_convert_fusion.13
  70.9 2.1 convolution_convert_fusion.14
  73.0 2.7 reshape.297
  75.7 1.6 reshape.298
  77.3 1.6 reshape.299
  78.8 4.6 fusion.115
  83.5 3.4 fusion.18
  86.9 1.9 fusion.15
  88.8 1.1 fusion.7
  91.3 1.0 fusion.16
  92.3 1.2 copy.315
  93.5 1.2 copy.290
  94.7 1.2 copy.316
  96.5 2.8 reshape.315
  99.3 2.2 reshape.302
  101.5 2.2 fusion.57
  103.7 3.0 reshape.316
  106.7 1.7 reshape.303
  108.4 1.4 copy.293
  110.9 1.7 convolution_add_fusion.3
  112.6 2.2 multiply_reduce_fusion.1
  115.0 1.3 fusion.49
  116.8 1.1 copy.299
  117.9 6.5 all-to-all-start.2
  124.4 1.3 convolution_bitcast_fusion.3
  125.7 1.3 convolution_bitcast_fusion.2
  127.0 1.4 copy.317
  128.5 1.2 copy.318
  129.7 2.2 reshape.318
  131.9 1.7 reshape.317
  133.6 1.4 convolution_bitcast_fusion.1
  135.1 1.3 convolution_bitcast_fusion
  136.4 2.4 pad_maximum_fusion.2
  138.8 1.1 copy.300
  140.1 1.4 convolution_convert_fusion.9
  142.4 2.3 fusion.12
  148.9 1.7 copy-done
  150.7 4.2 pad_maximum_fusion
  154.9 1.2 copy-done.4
  156.4 1.0 reshape.300
  157.4 1.4 fusion.26
  159.7 1.4 fusion.66
  161.1 1.4 convolution_add_fusion.1
  162.5 1.5 fusion.46
  164.9 1268.2 %reduce-scatter.2.cloned.1.call-done = f32[2,8,512]{2,1,0:T(8,128)} async-done(((f32[2,2048,512]{2,1,0:T(8,128)}), f32[2,8,512]{2,1,0:T(8,128)}) %reduce-scatter.2.cloned.1.call-update) | async-done | bytes 32784 | tf_op jit(solution)/shard_map/reduce_scatter | solution.py:174
  1433.1 1.4 broadcast_multiply_fusion
  (128 shorter events, 20.2 us)
Async XLA Ops:
  9.1 26.6 %all-to-all-start = ((s32[2,64,1]{0,2,1:T(1,128)}), s32[2,64,1]{0,2,1:T(1,128)S(1)}, u32[]{:S(2)}, u32[]{:S(2)}) async-start(s32[2,64,1]{0,2,1:T(1,128)} %broadcast_in_dim.86), calls=%async_computation | async-start | bytes 65536 | tf_op jit(solution)/shard_map/all_to_all | solution.py:140
  23.1 4.5 copy-start.6
  27.4 4.5 copy-start.25
  27.6 2.4 copy-start.27
  27.8 4.2 copy-start.10
  30.0 2.3 copy-start.2
  32.3 14.2 copy-start.12
  35.7 22.1 %all-to-all-start.1 = ((bf16[2,64,2,512]{3,2,0,1:T(2,128)(2,1)}), bf16[2,64,2,512]{3,2,0,1:T(2,128)(2,1)S(1)}, u32[]{:S(2)}, u32[]{:S(2)}) async-start(bf16[2,64,2,512]{3,2,0,1:T(2,128)(2,1)} %copy.268), calls=%async_computation.1 | async-start | bytes 524288 | tf_op jit(solution)/shard_map/all_to_all | solution.py:139
  67.4 0.7 copy-start.31
  83.4 3.5 copy-start.29
  83.5 3.4 copy-start.5
  83.5 3.4 copy-start.14
  88.8 1.2 copy-start.16
  88.8 1.3 copy-start.30
  90.1 1.2 copy-start.15
  94.7 1.5 copy-start.24
  110.9 4.1 copy-start.13
  115.0 9.4 copy-start.21
  116.3 9.4 copy-start.22
  117.9 20.9 %all-to-all-start.2 = ((bf16[2,64,2,512]{3,2,0,1:T(2,128)(2,1)}), bf16[2,64,2,512]{3,2,0,1:T(2,128)(2,1)}, u32[]{:S(2)}, u32[]{:S(2)}) async-start(bf16[2,64,2,512]{3,2,0,1:T(2,128)(2,1)} %copy.299), calls=%async_computation.2 | async-start | bytes 524288 | tf_op jit(solution)/shard_map/all_to_all | solution.py:163
  124.3 1308.7 %reduce-scatter.2.cloned.1.call-start = ((), (), s32[]{:S(2)}) async-start(), calls=%async_computation.4 | async-start | bytes 8421376 | tf_op jit(solution)/shard_map/reduce_scatter | solution.py:174
  125.7 2.8 copy-start.3
  133.6 2.7 copy-start.8
  133.6 2.7 copy-start.9
  139.9 2.4 copy-start.11
  142.3 2.4 copy-start.1
  142.3 2.4 copy-start.26
  144.7 1.0 copy-start.28
  145.7 0.8 copy-start.17
  145.7 1.4 copy-start.7
  146.2 1.6 copy-start.19
  147.1 1.1 copy-start.23
  148.5 2.2 copy-start
  154.9 1.2 copy-start.4
  156.3 3.3 copy-start.20
  156.3 4.7 copy-start.18
Sparse Core Ops, SparseCore 0:
  155.0 1278.0 reduce-scatter.1
where the time goes:
time: 1460 us; the launch traced here: 1440 us
  waiting for transfers between devices  1280 us (88%)
  matrix products  51.6 us (4%)
  local copies, waits for them, and re-layouts  50.1 us (3%)
  starting transfers between devices  28.6 us (2%)
  other arithmetic  19.5 us (1%)
  between operations  15.9 us (1%)
    reduce_scatter x1, waiting for transfers between devices, body(): lax.psum_scatter(stacked, ('scene', 'tile'), scatter_dimension=1, tiled=T...  1270 us
  transfers between devices with their start and end apart: 4, of which 2 were waited for; matrix products, arithmetic and copies ran while one was open for 3% of the time, Pallas kernels for 0%

commit v1 on v0

v1 whole, which is shorter than its diff:
```python
import functools

import jax
import jax.numpy as jnp
from jax import lax
from jax.experimental import pallas as pl
from jax.experimental.pallas import tpu as pltpu
from jax.sharding import PartitionSpec as P

MESH = pl.DeviceIdType.MESH
N_X, N_Y, N_Z, N_TILE = 4, 4, 8, 64
HEADS, HEAD_DIM = 16, 32
WIDTH, ROWS, HALF = 512, 256, 128
FRAMES = 8
GROUP = 4
EPSILON = 1e-06
SPATIAL, TEMPORAL = 0, 1
BF16, F32 = jnp.bfloat16, jnp.float32
EXP2_SCALE = HEAD_DIM ** (-0.5) * 1.4426950408889634
SCALE = HEAD_DIM ** (-0.5)
TAGS, STATES, GRADS, LAST, CORE, FIRST_X, FIRST_Y, SECOND_Y, SECOND_X = 0, 1, 2, 3, 4, 12, 14, 16, 18
N_SEM = 20


def dot(left, right):
    return jnp.dot(left, right, preferred_element_type=F32)


def dot_tn(left, right):
    return lax.dot_general(left, right, (((0,), (0,)), ((), ())), preferred_element_type=F32)


def dot_nt(left, right):
    return lax.dot_general(left, right, (((1,), (1,)), ((), ())), preferred_element_type=F32)


def iota(shape, axis):
    return lax.broadcasted_iota(jnp.int32, shape, axis)


def tile_index(y, z, core):
    return (y * N_Z + z) * 2 + core


def inverse_norm(rows):
    return lax.rsqrt(jnp.mean(rows * rows, axis=-1, keepdims=True) + EPSILON)


def kernel(
    position,
    frame,
    count,
    blocks,
    weights,
    cot,
    mixed_out,
    grad_out,
    weight_out,
    mask,
    tag_out,
    tag_in,
    spread,
    box_out,
    box_in,
    normed_t,
    query_t,
    key_t,
    value_t,
    key_n,
    value_n,
    context_t,
    soft_t,
    grad_context_t,
    grad_t,
    grid,
    parts,
    got_core,
    sum_a,
    sum_b,
    got_a,
    got_b,
    sum_a2,
    sum_b2,
    got_a2,
    got_b2,
    last,
    got_last,
    send_sem,
    recv_sem,
):
    x = lax.axis_index("scene")
    t = lax.axis_index("tile")
    core, z, y = lax.rem(t, 2), lax.rem(t // 2, N_Z), t // (2 * N_Z)
    peer_core = (x, tile_index(y, z, 1 - core))
    peers_x = [(lax.rem(x + d, N_X), t) for d in range(1, N_X)]
    peers_y = [(x, tile_index(lax.rem(y + d, N_Y), z, core)) for d in range(1, N_Y)]
    peers_z = [(x, tile_index(y, lax.rem(z + d, N_Z), core)) for d in range(1, N_Z)]

    barrier = pltpu.get_barrier_semaphore()

    @pl.loop(1, N_TILE)
    def _(d):
        pl.semaphore_signal(
            barrier, inc=1, device_id=(x, lax.rem(t + d, N_TILE)), device_id_type=MESH
        )

    for peer in peers_x:
        pl.semaphore_signal(barrier, inc=1, device_id=peer, device_id_type=MESH)

    def start(source, target, sem, peer):
        pltpu.make_async_remote_copy(
            src_ref=source,
            dst_ref=target,
            send_sem=send_sem.at[sem],
            recv_sem=recv_sem.at[sem],
            device_id=peer,
            device_id_type=MESH,
        ).start()

    def wait(sems, ref, sem):
        pltpu.make_async_copy(ref, ref, sems.at[sem]).wait()

    def send_all(outgoing, incoming, sem):
        @pl.loop(1, N_TILE)
        def _(d):
            to = lax.rem(t + d, N_TILE)
            start(outgoing(to), incoming.at[t], sem, (x, to))

    def project(piece, rows):
        scaled = (rows * inverse_norm(rows)).astype(BF16)
        normed_t[piece] = scaled.T
        first = 4 * piece
        query_t[piece] = dot(scaled, weights[first]).astype(BF16).T
        keys = dot(scaled, weights[first + 1]).astype(BF16)
        key_n[piece] = keys
        key_t[piece] = keys.T
        values = dot(scaled, weights[first + 2]).astype(BF16)
        value_n[piece] = values
        value_t[piece] = values.T

    def one_head(group_t, h):
        owner = iota((HALF, HALF), 0) // HEAD_DIM
        return jnp.where(owner == h, group_t, jnp.zeros_like(group_t))

    def attend(piece):
        @pl.loop(0, HEADS // GROUP)
        def _(g):
            feats = pl.ds(pl.multiple_of(g * HALF, HALF), HALF)
            for b in range(2):
                own = slice(b * HALF, (b + 1) * HALF)
                queries = query_t[piece, feats, own]
                keys = key_n[piece, own, feats]
                for h in range(GROUP):
                    scores = dot(keys, one_head(queries, h))
                    if piece == TEMPORAL:
                        scores = jnp.where(mask[...] > 0.5, scores, -1e30)
                    top = jnp.max(scores, axis=0, keepdims=True)
                    powers = jnp.exp2((scores - top) * EXP2_SCALE)
                    share = 1.0 / jnp.sum(powers, axis=0, keepdims=True)
                    soft = (powers * share).astype(BF16)
                    soft_t[piece, g, b, h] = soft
                    head = pl.ds(pl.multiple_of(g * HALF + h * HEAD_DIM, HEAD_DIM), HEAD_DIM)
                    context_t[piece, head, own] = dot(value_t[piece, head, own], soft).astype(BF16)

    def attend_back(piece):
        @pl.loop(0, HEADS // GROUP)
        def _(g):
            feats = pl.ds(pl.multiple_of(g * HALF, HALF), HALF)
            for b in range(2):
                own = slice(b * HALF, (b + 1) * HALF)
                grads = grad_context_t[piece, feats, own]
                values = value_n[piece, own, feats]
                for h in range(GROUP):
                    head = pl.ds(pl.multiple_of(g * HALF + h * HEAD_DIM, HEAD_DIM), HEAD_DIM)
                    soft = soft_t[piece, g, b, h]
                    wide = soft.astype(F32)
                    grad_soft = dot(values, one_head(grads, h))
                    mean = jnp.sum(wide * grad_soft, axis=0, keepdims=True)
                    grad_scores = (wide * (grad_soft - mean) * SCALE).astype(BF16)
                    grad_t[piece, 0, head, own] = dot(key_t[piece, head, own], grad_scores).astype(BF16)
                    grad_t[piece, 1, head, own] = dot_nt(query_t[piece, head, own], grad_scores).astype(BF16)
                    grad_t[piece, 2, head, own] = dot_nt(grad_context_t[piece, head, own], soft).astype(BF16)

    def input_back(piece, rows, rest):
        first = 4 * piece
        grad_normed_t = (
            dot(weights[first], grad_t[piece, 0])
            + dot(weights[first + 1], grad_t[piece, 1])
            + dot(weights[first + 2], grad_t[piece, 2])
        )
        grad_normed = grad_normed_t.T
        inverse = inverse_norm(rows)
        scaled = rows * inverse
        along = jnp.mean(scaled * grad_normed, axis=-1, keepdims=True)
        return rest.astype(F32) + inverse * (grad_normed - scaled * along)

    def put_part(piece, w, s, product):
        split = product.reshape(N_Y * N_Z, 2, 8, 2 * HALF)
        for c in range(2):
            unit = jnp.concatenate([split[:, c, :, :HALF], split[:, c, :, HALF:]], axis=1)
            parts[piece, c, w, s] = unit.astype(BF16).reshape(N_Y, N_Z, 16, HALF)

    def send_core(piece, w):
        start(parts.at[piece, 1 - core, w], got_core.at[piece, w], CORE + 4 * piece + w, peer_core)

    def context_sum(piece, rest):
        for s in range(2):
            put_part(piece, 3, s, dot(context_t[piece], rest[:, 2 * HALF * s : 2 * HALF * (s + 1)]))
        send_core(piece, 3)

    def normed_sums(piece):
        for w in range(3):
            for s in range(2):
                chunk = slice(2 * HALF * s, 2 * HALF * (s + 1))
                put_part(piece, w, s, dot_nt(normed_t[piece], grad_t[piece, w, chunk]))
            send_core(piece, w)

    def sum_core(piece):
        for w in range(4):
            wait(recv_sem, got_core.at[piece, w], CORE + 4 * piece + w)
            sum_a[piece, w] = (
                parts[piece, core, w, 0].astype(F32) + got_core[piece, w, 0].astype(F32)
            ).astype(BF16)
            for j in range(N_Y):
                sum_b[piece, j, w] = (
                    parts[piece, core, w, 1, j].astype(F32) + got_core[piece, w, 1, j].astype(F32)
                ).astype(BF16)
        for d in range(1, N_X):
            start(sum_a.at[piece, lax.rem(x + d, N_X)], got_a.at[piece, d - 1], FIRST_X + piece, peers_x[d - 1])
        for d in range(1, N_Y):
            start(sum_b.at[piece, lax.rem(y + d, N_Y)], got_b.at[piece, d - 1], FIRST_Y + piece, peers_y[d - 1])

    def add_up(own, got, n):
        total = own.astype(F32)
        for d in range(n - 1):
            total += got[d].astype(F32)
        return total

    def sum_first(piece):
        wait(recv_sem, got_a.at[piece], FIRST_X + piece)
        sum_a2[piece] = add_up(sum_a[piece, x], [got_a[piece, d] for d in range(N_X - 1)], N_X).astype(BF16)
        for d in range(1, N_Y):
            start(sum_a2.at[piece, lax.rem(y + d, N_Y)], got_a2.at[piece, d - 1], SECOND_Y + piece, peers_y[d - 1])
        wait(recv_sem, got_b.at[piece], FIRST_Y + piece)
        sum_b2[piece] = add_up(sum_b[piece, y], [got_b[piece, d] for d in range(N_Y - 1)], N_Y).astype(BF16)
        for d in range(1, N_X):
            start(sum_b2.at[piece, lax.rem(x + d, N_X)], got_b2.at[piece, d - 1], SECOND_X + piece, peers_x[d - 1])

    def sum_second(piece):
        wait(recv_sem, got_a2.at[piece], SECOND_Y + piece)
        last[:, piece, 0] = add_up(sum_a2[piece, y], [got_a2[piece, d] for d in range(N_Y - 1)], N_Y).astype(BF16)
        wait(recv_sem, got_b2.at[piece], SECOND_X + piece)
        last[:, piece, 1] = add_up(sum_b2[piece, x], [got_b2[piece, d] for d in range(N_X - 1)], N_X).astype(BF16)

    project(SPATIAL, blocks[...].astype(F32))

    lane = iota((1, HALF), 1)
    tags = [
        jnp.where(s < count[0, 0], position[0, s] * FRAMES + frame[0, s], -1) for s in range(2)
    ]
    tag_out[...] = jnp.where(lane < N_TILE, tags[0], tags[1])
    tag_in[t] = tag_out[...]
    pl.semaphore_wait(barrier, N_TILE - 1 + N_X - 1)
    send_all(lambda to: tag_out, tag_in, TAGS)

    attend(SPATIAL)
    states = blocks[...].astype(F32) + dot_tn(context_t[SPATIAL], weights[3])
    for s in range(2):
        for k in range(4):
            spread[pl.ds(4 * s + k, HALF, stride=8), :] = states[
                s * HALF : (s + 1) * HALF, k * HALF : (k + 1) * HALF
            ]
    box_out[0] = spread[...].astype(BF16).reshape(N_TILE, 16, HALF)
    box_in[0, t] = box_out[0, t]
    send_all(lambda to: box_out.at[0, to], box_in.at[0], STATES)

    wait(recv_sem, tag_in.at[pl.ds(0, N_TILE - 1)], TAGS)
    entry = iota((N_TILE, HALF), 1)
    placing = jnp.concatenate(
        [
            jnp.where(tag_in[:, 0, N_TILE * s : N_TILE * s + 1] == entry, 1.0, 0.0)
            for s in range(2)
        ],
        axis=0,
    ).astype(BF16)
    active = dot_tn(placing, jnp.ones((HALF, HALF), BF16))
    key_row, query_row = iota((HALF, HALF), 0), iota((HALF, HALF), 1)
    seen = (key_row // FRAMES == query_row // FRAMES) & (key_row <= query_row)
    mask[...] = jnp.where(seen, active, 0.0)
    active_wide = jnp.concatenate([active] * 4, axis=1) > 0.5
    natural = iota((ROWS, ROWS), 1)
    by_cell = iota((ROWS, ROWS), 0)
    order = jnp.where(
        natural == lax.rem(by_cell, HALF) * 2 + by_cell // HALF, 1.0, 0.0
    ).astype(BF16)
    cot_rows = dot(order, cot[...])
    rest = jnp.concatenate(
        [jnp.where(active_wide, cot_rows[j * HALF : (j + 1) * HALF], 0.0) for j in range(2)], axis=0
    ).astype(BF16)
    grad_context_t[TEMPORAL] = dot_nt(weights[7], rest).astype(BF16)

    wait(recv_sem, box_in.at[0, pl.ds(0, N_TILE - 1)], STATES)
    spread[...] = box_in[0].reshape(N_TILE * 16, HALF).astype(F32)
    for j in range(2):
        rows = jnp.concatenate(
            [
                jnp.concatenate(
                    [spread[pl.ds(8 * j + 4 * s + k, N_TILE, stride=16), :] for k in range(4)], axis=1
                )
                for s in range(2)
            ],
            axis=0,
        ).astype(BF16)
        grid[j * HALF : (j + 1) * HALF] = dot_tn(placing, rows)

    project(TEMPORAL, grid[...])
    attend(TEMPORAL)
    attend_back(TEMPORAL)
    grid_grad = input_back(TEMPORAL, grid[...], rest).astype(BF16)
    for j in range(2):
        back = dot(placing, grid_grad[j * HALF : (j + 1) * HALF])
        for s in range(2):
            for k in range(4):
                spread[pl.ds(8 * j + 4 * s + k, N_TILE, stride=16), :] = back[
                    s * N_TILE : (s + 1) * N_TILE, k * HALF : (k + 1) * HALF
                ]
    box_out[1] = spread[...].astype(BF16).reshape(N_TILE, 16, HALF)
    box_in[1, t] = box_out[1, t]
    send_all(lambda to: box_out.at[1, to], box_in.at[1], GRADS)

    context_sum(TEMPORAL, rest)
    normed_sums(TEMPORAL)
    temporal = grid[...] + dot_tn(context_t[TEMPORAL], weights[7])
    mixed = jnp.concatenate(
        [jnp.where(active_wide, temporal[j * HALF : (j + 1) * HALF], 0.0) for j in range(2)], axis=0
    ).astype(BF16)
    mixed_out[...] = dot_tn(order, mixed).astype(BF16)

    wait(recv_sem, box_in.at[1, pl.ds(0, N_TILE - 1)], GRADS)
    spread[...] = box_in[1].reshape(N_TILE * 16, HALF).astype(F32)
    rest = jnp.concatenate(
        [
            jnp.concatenate([spread[pl.ds(4 * s + k, HALF, stride=8), :] for k in range(4)], axis=1)
            for s in range(2)
        ],
        axis=0,
    ).astype(BF16)
    context_sum(SPATIAL, rest)
    grad_context_t[SPATIAL] = dot_nt(weights[3], rest).astype(BF16)
    sum_core(TEMPORAL)
    attend_back(SPATIAL)
    normed_sums(SPATIAL)
    sum_first(TEMPORAL)
    sum_core(SPATIAL)
    grad_out[...] = input_back(SPATIAL, blocks[...].astype(F32), rest).astype(BF16)
    sum_second(TEMPORAL)
    sum_first(SPATIAL)
    sum_second(SPATIAL)
    for d in range(1, N_Z):
        start(last.at[lax.rem(z + d, N_Z)], got_last.at[d - 1], LAST, peers_z[d - 1])
    wait(recv_sem, got_last, LAST)
    scaling = (N_X * N_TILE * ROWS) ** (-0.5)
    total = add_up(last[z], [got_last[d] for d in range(N_Z - 1)], N_Z) * scaling
    for piece in range(2):
        for s in range(2):
            for half in range(2):
                column = (2 * s + half) * HALF
                weight_out[piece, :, column : column + HALF] = total[piece, s, 8 * half : 8 * half + 8]

    wait(send_sem, tag_in.at[pl.ds(0, N_TILE - 1)], TAGS)
    wait(send_sem, box_in.at[0, pl.ds(0, N_TILE - 1)], STATES)
    wait(send_sem, box_in.at[1, pl.ds(0, N_TILE - 1)], GRADS)
    wait(send_sem, got_last, LAST)
    for piece in range(2):
        for w in range(4):
            wait(send_sem, got_core.at[piece, w], CORE + 4 * piece + w)
        wait(send_sem, got_a.at[piece], FIRST_X + piece)
        wait(send_sem, got_b.at[piece], FIRST_Y + piece)
        wait(send_sem, got_a2.at[piece], SECOND_Y + piece)
        wait(send_sem, got_b2.at[piece], SECOND_X + piece)


def body(blocks, block_position, block_frame, block_count, weights, cotangent):
    unit = (16, HALF)
    pair = (2, ROWS, WIDTH)
    turned = (2, WIDTH, ROWS)
    vmem = pl.BlockSpec(memory_space=pltpu.VMEM)
    smem = pl.BlockSpec(memory_space=pltpu.SMEM)
    mixed, input_grad, weight_grad = pl.pallas_call(
        kernel,
        out_shape=(
            jax.ShapeDtypeStruct((ROWS, WIDTH), BF16),
            jax.ShapeDtypeStruct((ROWS, WIDTH), BF16),
            jax.ShapeDtypeStruct((2, 8, WIDTH), F32),
        ),
        in_specs=[smem, smem, smem, vmem, vmem, vmem],
        out_specs=(vmem, vmem, vmem),
        scratch_shapes=[
            pltpu.VMEM((HALF, HALF), F32),
            pltpu.VMEM((1, HALF), jnp.int32),
            pltpu.VMEM((N_TILE, 1, HALF), jnp.int32),
            pltpu.VMEM((N_TILE * 16, HALF), F32),
            pltpu.VMEM((2, N_TILE) + unit, BF16),
            pltpu.VMEM((2, N_TILE) + unit, BF16),
            pltpu.VMEM(turned, BF16),
            pltpu.VMEM(turned, BF16),
            pltpu.VMEM(turned, BF16),
            pltpu.VMEM(turned, BF16),
            pltpu.VMEM(pair, BF16),
            pltpu.VMEM(pair, BF16),
            pltpu.VMEM(turned, BF16),
            pltpu.VMEM((2, HEADS // GROUP, 2, GROUP, HALF, HALF), BF16),
            pltpu.VMEM(turned, BF16),
            pltpu.VMEM((2, 3, WIDTH, ROWS), BF16),
            pltpu.VMEM((ROWS, WIDTH), F32),
            pltpu.VMEM((2, 2, 4, 2, N_Y, N_Z) + unit, BF16),
            pltpu.VMEM((2, 4, 2, N_Y, N_Z) + unit, BF16),
            pltpu.VMEM((2, N_X, N_Y, N_Z) + unit, BF16),
            pltpu.VMEM((2, N_Y, N_X, N_Z) + unit, BF16),
            pltpu.VMEM((2, N_X - 1, N_Y, N_Z) + unit, BF16),
            pltpu.VMEM((2, N_Y - 1, N_X, N_Z) + unit, BF16),
            pltpu.VMEM((2, N_Y, N_Z) + unit, BF16),
            pltpu.VMEM((2, N_X, N_Z) + unit, BF16),
            pltpu.VMEM((2, N_Y - 1, N_Z) + unit, BF16),
            pltpu.VMEM((2, N_X - 1, N_Z) + unit, BF16),
            pltpu.VMEM((N_Z, 2, 2) + unit, BF16),
            pltpu.VMEM((N_Z - 1, 2, 2) + unit, BF16),
            pltpu.SemaphoreType.DMA((N_SEM,)),
            pltpu.SemaphoreType.DMA((N_SEM,)),
        ],
        compiler_params=pltpu.CompilerParams(
            collective_id=0, has_side_effects=True, vmem_limit_bytes=48 * 1024 * 1024
        ),
    )(
        block_position,
        block_frame,
        block_count,
        blocks.reshape(ROWS, WIDTH),
        weights,
        cotangent.reshape(ROWS, WIDTH),
    )
    return mixed.reshape(cotangent.shape), input_grad.reshape(blocks.shape), weight_grad


def solution(mesh):
    return jax.shard_map(
        body,
        mesh=mesh,
        in_specs=(
            P("scene", "tile", None, None),
            P("scene", "tile"),
            P("scene", "tile"),
            P("scene", "tile"),
            P(),
            P("scene", None, None, "tile", None),
        ),
        out_specs=(
            P("scene", None, None, "tile", None),
            P("scene", "tile", None, None),
            P(None, ("scene", "tile"), None),
        ),
        check_vma=False,
    )
```

time: 1460 us -> 82 us (0.06); the launches traced: 1440 us -> 81.8 us
  waiting for transfers between devices: 1280 us -> 0 us
  Pallas kernels: 0 us -> 72.9 us
  matrix products: 51.6 us -> 0 us
  local copies, waits for them, and re-layouts: 50.1 us -> 7.61 us
  starting transfers between devices: 28.6 us -> 0 us
  other arithmetic: 19.5 us -> 0 us
  between operations: 15.9 us -> 1.3 us
    reduce_scatter x1 -> x0, waiting for transfers between devices: 1270 us -> none  [body(): lax.psum_scatter(stacked, ('scene', 'tile'), scatter_dimension=1, tiled=T...]
    pallas_call x0 -> x1, Pallas kernels: none -> 72.9 us  [body(): pl.pallas_call(kernel, out_shape=(jax.ShapeDtypeStruct((ROWS, WIDTH), BF1...]
    dot_general x36 -> x0, matrix products: 44.8 us -> none  [the longest x8 13.1 us: right_dot_t(): lax.dot_general(grad_rows, weight, (((grad_rows.ndim - 1,), (1,)), ((), (...]
    all_to_all x3 -> x0, starting transfers between devices: 28.5 us -> none  [the longest x1 11.8 us: body(): lax.all_to_all(tag_rows, 'tile', split_axis=1, concat_axis=1, tiled=True)]
    reshape x15 -> x2, local copies, waits for them, and re-layouts: 23.2 us -> 1.86 us  [the longest x1 1.05 us: body(): cotangent.reshape(ROWS, WIDTH)]
  transfers between devices with their start and end apart: 4 -> 0, of which waited for: 2 -> 0; matrix products, arithmetic and copies ran while one was open for 3% -> 0% of each run, Pallas kernels for 0% -> 0%
where the time goes in v1:
time: 82 us; the launch traced here: 81.8 us
  Pallas kernels  72.9 us (89%)
  local copies, waits for them, and re-layouts  7.61 us (9%)
  between operations  1.3 us (2%)
    pallas_call x1, Pallas kernels, body(): pl.pallas_call(kernel, out_shape=(jax.ShapeDtypeStruct((ROWS, WIDTH), BF1...  72.9 us
    unnamed x10, local copies, waits for them, and re-layouts  5.76 us

profile of v1, /device:TPU:32, one launch (start us, length us, event | category | flops | bytes accessed | tf_op | source)
XLA Modules:
  0.0 81.8 jit_solution(15719259299984948919)
XLA Ops:
  1.3 1.1 %reshape.19.cot = bf16[256,512]{1,0:T(8,128)(2,1)S(1)} reshape(bf16[1,16,8,2,512]{4,3,2,1,0:T(2,128)(2,1)} %param.11) | data formatting | bytes 524288 | tf_op jit(solution)/shard_map/reshape | solution.py:440
  2.3 0.0 copy-start
  2.3 2.2 %copy-done = bf16[8,512,512]{2,1,0:T(8,128)(2,1)S(1)} copy-done((bf16[8,512,512]{2,1,0:T(8,128)(2,1)S(1)}, bf16[8,512,512]{2,1,0:T(8,128)(2,1)}, u32[]{:S(2)}) %copy-start) | copy-done | bytes 4194328
  4.5 0.0 copy-start.1
  4.5 0.9 %copy-done.1 = bf16[1,2,128,512]{3,2,1,0:T(8,128)(2,1)S(1)} copy-done((bf16[1,2,128,512]{3,2,1,0:T(8,128)(2,1)S(1)}, bf16[1,2,128,512]{3,2,1,0:T(8,128)(2,1)}, u32[]{:S(2)}) %copy-start.1) | copy-done | bytes 262168
  5.5 0.0 copy-start.2
  5.5 0.7 copy-done.2
  6.1 0.0 copy-start.3
  6.1 0.7 copy-done.3
  6.8 72.9 %shard_map.85 = (bf16[256,512]{1,0:T(8,128)(2,1)S(1)}, bf16[256,512]{1,0:T(8,128)(2,1)S(1)}, f32[2,8,512]{2,1,0:T(8,128)S(1)}) custom-call(s32[1,2]{1,0:T(1,128)S(1)} %copy-done.2, s32[1,2]{1,0:T(1,128)S(1)} %copy-done.3, s32[1,1]{1,0:T(1,128)S(6)} %copy.11.count, bf16[256,512]{1,0:T(8,128)(2,1)S(1)} %bitcast.2, bf16[8,512,512]{2,1,0:T(8,128)(2,1)S(1)} %copy-done, ...), custom_call_target="tpu_custom_call" | custom-call | tf_op jit(solution)/shard_map/pallas_call | solution.py:389
  79.7 0.8 reshape.20
  80.5 0.7 copy.12
  81.2 0.6 copy.13
Async XLA Ops:
  2.3 2.2 %copy-start = (bf16[8,512,512]{2,1,0:T(8,128)(2,1)S(1)}, bf16[8,512,512]{2,1,0:T(8,128)(2,1)}, u32[]{:S(2)}) copy-start(bf16[8,512,512]{2,1,0:T(8,128)(2,1)} %weights.1) | copy-start | bytes 12582916
  4.5 0.9 %copy-start.1 = (bf16[1,2,128,512]{3,2,1,0:T(8,128)(2,1)S(1)}, bf16[1,2,128,512]{3,2,1,0:T(8,128)(2,1)}, u32[]{:S(2)}) copy-start(bf16[1,2,128,512]{3,2,1,0:T(8,128)(2,1)} %param.6) | copy-start | bytes 786436
  5.5 0.7 copy-start.2
  6.1 0.7 copy-start.3

commit v2 on v1

v2 whole, which is shorter than its diff:
```python
import functools

import jax
import jax.numpy as jnp
from jax import lax
from jax.experimental import pallas as pl
from jax.experimental.pallas import tpu as pltpu
from jax.sharding import PartitionSpec as P

MESH = pl.DeviceIdType.MESH
N_X, N_Y, N_Z, N_TILE = 4, 4, 8, 64
HEADS, HEAD_DIM = 16, 32
WIDTH, ROWS, HALF = 512, 256, 128
FRAMES = 8
GROUP = 4
EPSILON = 1e-06
SPATIAL, TEMPORAL = 0, 1
BF16, F32 = jnp.bfloat16, jnp.float32
EXP2_SCALE = HEAD_DIM ** (-0.5) * 1.4426950408889634
SCALE = HEAD_DIM ** (-0.5)
TAGS, STATES, GRADS, CORE, FIRST_X, FIRST_Y, SECOND_Y, SECOND_X, LAST = 0, 1, 2, 3, 11, 13, 15, 17, 19
N_SEM = 21


def dot(left, right):
    return jnp.dot(left, right, preferred_element_type=F32)


def dot_tn(left, right):
    return lax.dot_general(left, right, (((0,), (0,)), ((), ())), preferred_element_type=F32)


def dot_nt(left, right):
    return lax.dot_general(left, right, (((1,), (1,)), ((), ())), preferred_element_type=F32)


def iota(shape, axis):
    return lax.broadcasted_iota(jnp.int32, shape, axis)


def tile_index(y, z, core):
    return (y * N_Z + z) * 2 + core


def inverse_norm(rows):
    return lax.rsqrt(jnp.mean(rows * rows, axis=-1, keepdims=True) + EPSILON)


def kernel(
    position_in,
    frame_in,
    count_in,
    blocks_in,
    weights_in,
    cot_in,
    mixed_to,
    grad_to,
    weight_to,
    mixed_out,
    grad_out,
    weight_out,
    position,
    frame,
    count,
    blocks,
    weights,
    weights_t,
    cot,
    mask,
    tag_out,
    tag_in,
    spread,
    box_out,
    box_in,
    normed_n,
    normed_t,
    query_n,
    query_t,
    key_n,
    key_t,
    value_n,
    value_t,
    context_t,
    soft_t,
    grad_context_n,
    grad_context_t,
    grad_n,
    grid,
    parts,
    got_core,
    sum_a,
    sum_b,
    got_a,
    got_b,
    sum_a2,
    sum_b2,
    got_a2,
    got_b2,
    last,
    got_last,
    in_sem,
    out_sem,
    send_sem,
    recv_sem,
):
    loads = [
        pltpu.make_async_copy(source, target, in_sem.at[i])
        for i, (source, target) in enumerate(
            [
                (blocks_in, blocks),
                (weights_in.at[pl.ds(0, 3)], weights.at[pl.ds(0, 3)]),
                (position_in, position),
                (frame_in, frame),
                (count_in, count),
                (weights_in.at[pl.ds(3, 5)], weights.at[pl.ds(3, 5)]),
                (cot_in, cot),
            ]
        )
    ]
    for load in loads:
        load.start()
    stores = [
        pltpu.make_async_copy(source, target, out_sem.at[i])
        for i, (source, target) in enumerate(
            [(mixed_out, mixed_to), (grad_out, grad_to), (weight_out, weight_to)]
        )
    ]

    x = lax.axis_index("scene")
    t = lax.axis_index("tile")
    core, z, y = lax.rem(t, 2), lax.rem(t // 2, N_Z), t // (2 * N_Z)
    peer_core = (x, tile_index(y, z, 1 - core))
    peers_x = [(lax.rem(x + d, N_X), t) for d in range(1, N_X)]
    peers_y = [(x, tile_index(lax.rem(y + d, N_Y), z, core)) for d in range(1, N_Y)]
    peers_z = [(x, tile_index(y, lax.rem(z + d, N_Z), core)) for d in range(1, N_Z)]

    barrier = pltpu.get_barrier_semaphore()

    @pl.loop(1, N_TILE)
    def _(d):
        pl.semaphore_signal(
            barrier, inc=1, device_id=(x, lax.rem(t + d, N_TILE)), device_id_type=MESH
        )

    for peer in peers_x:
        pl.semaphore_signal(barrier, inc=1, device_id=peer, device_id_type=MESH)

    def start(source, target, sem, peer):
        pltpu.make_async_remote_copy(
            src_ref=source,
            dst_ref=target,
            send_sem=send_sem.at[sem],
            recv_sem=recv_sem.at[sem],
            device_id=peer,
            device_id_type=MESH,
        ).start()

    def wait(sems, ref, sem):
        pltpu.make_async_copy(ref, ref, sems.at[sem]).wait()

    def send_all(outgoing, incoming, sem):
        @pl.loop(1, N_TILE)
        def _(d):
            to = lax.rem(t + d, N_TILE)
            start(outgoing(to), incoming.at[t], sem, (x, to))

    def project(piece, rows):
        scaled = (rows * inverse_norm(rows)).astype(BF16)
        normed_n[piece] = scaled
        first = 4 * piece
        queries = dot(scaled, weights[first]).astype(BF16)
        query_n[piece] = queries
        query_t[...] = queries.T
        key_n[piece] = dot(scaled, weights[first + 1]).astype(BF16)
        values = dot(scaled, weights[first + 2]).astype(BF16)
        value_n[piece] = values
        value_t[...] = values.T

    def one_head(rows, h, axis):
        owner = iota((HALF, HALF), axis) // HEAD_DIM
        return jnp.where(owner == h, rows, jnp.zeros_like(rows))

    def by_head(rows, axis):
        return jnp.concatenate([one_head(rows, h, axis) for h in range(GROUP)], axis=1 - axis)

    def attend(piece):
        @pl.loop(0, HEADS // GROUP)
        def _(g):
            feats = pl.ds(pl.multiple_of(g * HALF, HALF), HALF)
            for b in range(2):
                own = slice(b * HALF, (b + 1) * HALF)
                queries = query_t[feats, own]
                keys = key_n[piece, own, feats]
                for h in range(GROUP):
                    scores = dot(keys, one_head(queries, h, 0))
                    if piece == TEMPORAL:
                        scores = jnp.where(mask[...] > 0.5, scores, -1e30)
                    top = jnp.max(scores, axis=0, keepdims=True)
                    powers = jnp.exp2((scores - top) * EXP2_SCALE)
                    share = 1.0 / jnp.sum(powers, axis=0, keepdims=True)
                    soft = (powers * share).astype(BF16)
                    soft_t[piece, g, b, :, h * HALF : (h + 1) * HALF] = soft
                    head = pl.ds(pl.multiple_of(g * HALF + h * HEAD_DIM, HEAD_DIM), HEAD_DIM)
                    context_t[piece, head, own] = dot(value_t[head, own], soft).astype(BF16)

    def attend_back(piece, lower, upper):
        @pl.loop(lower, upper)
        def _(g):
            feats = pl.ds(pl.multiple_of(g * HALF, HALF), HALF)
            for b in range(2):
                own = slice(b * HALF, (b + 1) * HALF)
                grads_t = grad_context_t[feats, own]
                values = value_n[piece, own, feats]
                soft = soft_t[piece, g, b]
                grad_scores, grad_queries = [], []
                for h in range(GROUP):
                    wide = soft[:, h * HALF : (h + 1) * HALF].astype(F32)
                    grad_soft = dot(values, one_head(grads_t, h, 0))
                    mean = jnp.sum(wide * grad_soft, axis=0, keepdims=True)
                    grad_scores.append((wide * (grad_soft - mean)).astype(BF16))
                    head = pl.ds(pl.multiple_of(g * HALF + h * HEAD_DIM, HEAD_DIM), HEAD_DIM)
                    grad_queries.append(dot(key_t[piece, head, own], grad_scores[h]))
                grad_queries = jnp.concatenate(grad_queries, axis=0)
                grad_n[piece, 0, own, feats] = (grad_queries * SCALE).T.astype(BF16)
                grad_keys = dot(
                    jnp.concatenate(grad_scores, axis=1), by_head(query_n[piece, own, feats], 1)
                )
                grad_n[piece, 1, own, feats] = (grad_keys * SCALE).astype(BF16)
                grad_values = dot(soft, by_head(grad_context_n[own, feats], 1))
                grad_n[piece, 2, own, feats] = grad_values.astype(BF16)

    def context_back(piece, rest):
        grads = dot(rest, weights_t[4 * piece + 3]).astype(BF16)
        grad_context_n[...] = grads
        grad_context_t[...] = grads.T

    def input_back(piece, rows, rest):
        first = 4 * piece
        grad_normed = (
            dot(grad_n[piece, 0], weights_t[first])
            + dot(grad_n[piece, 1], weights_t[first + 1])
            + dot(grad_n[piece, 2], weights_t[first + 2])
        )
        inverse = inverse_norm(rows)
        scaled = rows * inverse
        along = jnp.mean(scaled * grad_normed, axis=-1, keepdims=True)
        return rest.astype(F32) + inverse * (grad_normed - scaled * along)

    def put_part(piece, w, s, product):
        split = product.reshape(N_Y * N_Z, 2, 8, 2 * HALF)
        for c in range(2):
            unit = jnp.concatenate([split[:, c, :, :HALF], split[:, c, :, HALF:]], axis=1)
            parts[piece, c, s, w] = unit.astype(BF16).reshape(N_Y, N_Z, 16, HALF)

    def core_parts(s, output):
        return (s, 3) if output else (s, pl.ds(0, 3))

    def core_sem(piece, s, output):
        return CORE + 4 * piece + 2 * s + output

    def send_core(piece, s, output):
        at = core_parts(s, output)
        start(
            parts.at[(piece, 1 - core) + at],
            got_core.at[(piece,) + at],
            core_sem(piece, s, output),
            peer_core,
        )

    def context_sum(piece, rest):
        for s in range(2):
            put_part(piece, 3, s, dot(context_t[piece], rest[:, 2 * HALF * s : 2 * HALF * (s + 1)]))
            send_core(piece, s, 1)

    def normed_sum(piece, s):
        chunk = slice(2 * HALF * s, 2 * HALF * (s + 1))
        for w in range(3):
            put_part(piece, w, s, dot(normed_t[piece], grad_n[piece, w, :, chunk]))
        send_core(piece, s, 0)

    def sum_core(piece, s):
        for output in (1, 0):
            wait(recv_sem, got_core.at[(piece,) + core_parts(s, output)], core_sem(piece, s, output))
        for w in range(4):
            for j in range(N_Y):
                total = (
                    parts[piece, core, s, w, j].astype(F32) + got_core[piece, s, w, j].astype(F32)
                ).astype(BF16)
                if s == 0:
                    sum_a[piece, w, j] = total
                else:
                    sum_b[piece, j, w] = total
        if s == 0:
            for d in range(1, N_X):
                start(sum_a.at[piece, lax.rem(x + d, N_X)], got_a.at[piece, d - 1], FIRST_X + piece, peers_x[d - 1])
        else:
            for d in range(1, N_Y):
                start(sum_b.at[piece, lax.rem(y + d, N_Y)], got_b.at[piece, d - 1], FIRST_Y + piece, peers_y[d - 1])

    def add_up(own, got, n):
        total = own.astype(F32)
        for d in range(n - 1):
            total += got[d].astype(F32)
        return total

    def sum_first(piece, s):
        if s == 0:
            wait(recv_sem, got_a.at[piece], FIRST_X + piece)
            sum_a2[piece] = add_up(sum_a[piece, x], [got_a[piece, d] for d in range(N_X - 1)], N_X).astype(BF16)
            for d in range(1, N_Y):
                start(sum_a2.at[piece, lax.rem(y + d, N_Y)], got_a2.at[piece, d - 1], SECOND_Y + piece, peers_y[d - 1])
        else:
            wait(recv_sem, got_b.at[piece], FIRST_Y + piece)
            sum_b2[piece] = add_up(sum_b[piece, y], [got_b[piece, d] for d in range(N_Y - 1)], N_Y).astype(BF16)
            for d in range(1, N_X):
                start(sum_b2.at[piece, lax.rem(x + d, N_X)], got_b2.at[piece, d - 1], SECOND_X + piece, peers_x[d - 1])

    def sum_second(piece):
        wait(recv_sem, got_a2.at[piece], SECOND_Y + piece)
        last[piece, :, 0] = add_up(sum_a2[piece, y], [got_a2[piece, d] for d in range(N_Y - 1)], N_Y).astype(BF16)
        wait(recv_sem, got_b2.at[piece], SECOND_X + piece)
        last[piece, :, 1] = add_up(sum_b2[piece, x], [got_b2[piece, d] for d in range(N_X - 1)], N_X).astype(BF16)
        for d in range(1, N_Z):
            start(last.at[piece, lax.rem(z + d, N_Z)], got_last.at[piece, d - 1], LAST + piece, peers_z[d - 1])

    def sum_last(piece):
        wait(recv_sem, got_last.at[piece], LAST + piece)
        scaling = (N_X * N_TILE * ROWS) ** (-0.5)
        total = add_up(last[piece, z], [got_last[piece, d] for d in range(N_Z - 1)], N_Z) * scaling
        for s in range(2):
            for half in range(2):
                column = (2 * s + half) * HALF
                weight_out[piece, :, column : column + HALF] = total[s, 8 * half : 8 * half + 8]

    loads[0].wait()
    loads[1].wait()
    project(SPATIAL, blocks[...].astype(F32))

    lane = iota((1, HALF), 1)
    for i in range(2, 5):
        loads[i].wait()
    usable = iota((1, 2), 1) < count[:, 0:1]
    tags = jnp.where(usable, position[...] * FRAMES + frame[...], -1)
    tag_out[...] = jnp.where(lane < N_TILE, tags[:, 0:1], tags[:, 1:2])
    tag_in[t] = tag_out[...]
    pl.semaphore_wait(barrier, N_TILE - 1 + N_X - 1)
    send_all(lambda to: tag_out, tag_in, TAGS)

    attend(SPATIAL)
    loads[5].wait()
    states = blocks[...].astype(F32) + dot_tn(context_t[SPATIAL], weights[3])
    for s in range(2):
        for k in range(4):
            spread[pl.ds(4 * s + k, HALF, stride=8), :] = states[
                s * HALF : (s + 1) * HALF, k * HALF : (k + 1) * HALF
            ]
    box_out[0] = spread[...].astype(BF16).reshape(N_TILE, 16, HALF)
    box_in[0, t] = box_out[0, t]
    send_all(lambda to: box_out.at[0, to], box_in.at[0], STATES)

    for w in range(8):
        weights_t[w] = weights[w].T
    normed_t[SPATIAL] = normed_n[SPATIAL].T
    key_t[SPATIAL] = key_n[SPATIAL].T

    wait(recv_sem, tag_in.at[pl.ds(0, N_TILE - 1)], TAGS)
    entry = iota((N_TILE, HALF), 1)
    placing = jnp.concatenate(
        [
            jnp.where(tag_in[:, 0, N_TILE * s : N_TILE * s + 1] == entry, 1.0, 0.0)
            for s in range(2)
        ],
        axis=0,
    ).astype(BF16)
    active = dot_tn(placing, jnp.ones((HALF, HALF), BF16))
    key_row, query_row = iota((HALF, HALF), 0), iota((HALF, HALF), 1)
    seen = (key_row // FRAMES == query_row // FRAMES) & (key_row <= query_row)
    mask[...] = jnp.where(seen, active, 0.0)
    active_wide = jnp.concatenate([active] * 4, axis=1) > 0.5
    loads[6].wait()
    rest = jnp.concatenate(
        [jnp.where(active_wide, cot[:, j, :].astype(F32), 0.0) for j in range(2)], axis=0
    ).astype(BF16)
    context_back(TEMPORAL, rest)

    wait(recv_sem, box_in.at[0, pl.ds(0, N_TILE - 1)], STATES)
    spread[...] = box_in[0].reshape(N_TILE * 16, HALF).astype(F32)
    for j in range(2):
        rows = jnp.concatenate(
            [
                jnp.concatenate(
                    [spread[pl.ds(8 * j + 4 * s + k, N_TILE, stride=16), :] for k in range(4)], axis=1
                )
                for s in range(2)
            ],
            axis=0,
        ).astype(BF16)
        grid[j * HALF : (j + 1) * HALF] = dot_tn(placing, rows)

    project(TEMPORAL, grid[...])
    key_t[TEMPORAL] = key_n[TEMPORAL].T
    attend(TEMPORAL)
    attend_back(TEMPORAL, 0, HEADS // GROUP)
    grid_grad = input_back(TEMPORAL, grid[...], rest).astype(BF16)
    for j in range(2):
        back = dot(placing, grid_grad[j * HALF : (j + 1) * HALF])
        for s in range(2):
            for k in range(4):
                spread[pl.ds(8 * j + 4 * s + k, N_TILE, stride=16), :] = back[
                    s * N_TILE : (s + 1) * N_TILE, k * HALF : (k + 1) * HALF
                ]
    box_out[1] = spread[...].astype(BF16).reshape(N_TILE, 16, HALF)
    box_in[1, t] = box_out[1, t]
    send_all(lambda to: box_out.at[1, to], box_in.at[1], GRADS)

    context_sum(TEMPORAL, rest)
    normed_t[TEMPORAL] = normed_n[TEMPORAL].T
    normed_sum(TEMPORAL, 0)
    normed_sum(TEMPORAL, 1)
    temporal = grid[...] + dot_tn(context_t[TEMPORAL], weights[7])
    for j in range(2):
        mixed_out[:, j, :] = jnp.where(active_wide, temporal[j * HALF : (j + 1) * HALF], 0.0).astype(BF16)
    stores[0].start()
    sum_core(TEMPORAL, 0)
    sum_core(TEMPORAL, 1)

    wait(recv_sem, box_in.at[1, pl.ds(0, N_TILE - 1)], GRADS)
    spread[...] = box_in[1].reshape(N_TILE * 16, HALF).astype(F32)
    rest = jnp.concatenate(
        [
            jnp.concatenate([spread[pl.ds(4 * s + k, HALF, stride=8), :] for k in range(4)], axis=1)
            for s in range(2)
        ],
        axis=0,
    ).astype(BF16)
    context_sum(SPATIAL, rest)
    context_back(SPATIAL, rest)
    attend_back(SPATIAL, 0, 2)
    normed_sum(SPATIAL, 0)
    sum_first(TEMPORAL, 0)
    sum_first(TEMPORAL, 1)
    attend_back(SPATIAL, 2, 4)
    normed_sum(SPATIAL, 1)
    sum_core(SPATIAL, 0)
    sum_second(TEMPORAL)
    sum_core(SPATIAL, 1)
    grad_out[...] = input_back(SPATIAL, blocks[...].astype(F32), rest).astype(BF16)
    stores[1].start()
    sum_first(SPATIAL, 0)
    sum_first(SPATIAL, 1)
    sum_last(TEMPORAL)
    sum_second(SPATIAL)
    sum_last(SPATIAL)
    stores[2].start()

    wait(send_sem, tag_in.at[pl.ds(0, N_TILE - 1)], TAGS)
    wait(send_sem, box_in.at[0, pl.ds(0, N_TILE - 1)], STATES)
    wait(send_sem, box_in.at[1, pl.ds(0, N_TILE - 1)], GRADS)
    for piece in range(2):
        for s in range(2):
            for output in range(2):
                wait(send_sem, got_core.at[(piece,) + core_parts(s, output)], core_sem(piece, s, output))
        wait(send_sem, got_a.at[piece], FIRST_X + piece)
        wait(send_sem, got_b.at[piece], FIRST_Y + piece)
        wait(send_sem, got_a2.at[piece], SECOND_Y + piece)
        wait(send_sem, got_b2.at[piece], SECOND_X + piece)
        wait(send_sem, got_last.at[piece], LAST + piece)
    for store in stores:
        store.wait()


def hand_over(*refs):
    sources, targets, held, sem_in, sem_out = refs[:3], refs[3:6], refs[6:9], refs[9], refs[10]
    loads = [pltpu.make_async_copy(sources[i], held[i], sem_in.at[i]) for i in range(3)]
    stores = [pltpu.make_async_copy(held[i], targets[i], sem_out.at[i]) for i in range(3)]
    for load in loads:
        load.start()
    for load, store in zip(loads, stores):
        load.wait()
        store.start()
    for store in stores:
        store.wait()


def body(blocks, block_position, block_frame, block_count, weights, cotangent):
    unit = (16, HALF)
    pair = (2, ROWS, WIDTH)
    turned = (2, WIDTH, ROWS)
    hbm = pl.BlockSpec(memory_space=pltpu.HBM)
    out_shape = (
        jax.ShapeDtypeStruct((HALF, 2, WIDTH), BF16),
        jax.ShapeDtypeStruct((ROWS, WIDTH), BF16),
        jax.ShapeDtypeStruct((2, 8, WIDTH), F32),
    )
    results = pl.pallas_call(
        kernel,
        out_shape=out_shape,
        in_specs=[hbm] * 6,
        out_specs=(hbm, hbm, hbm),
        scratch_shapes=[
            pltpu.VMEM((HALF, 2, WIDTH), BF16),
            pltpu.VMEM((ROWS, WIDTH), BF16),
            pltpu.VMEM((2, 8, WIDTH), F32),
            pltpu.VMEM((1, 2), jnp.int32),
            pltpu.VMEM((1, 2), jnp.int32),
            pltpu.VMEM((1, 1), jnp.int32),
            pltpu.VMEM((ROWS, WIDTH), BF16),
            pltpu.VMEM((8, WIDTH, WIDTH), BF16),
            pltpu.VMEM((8, WIDTH, WIDTH), BF16),
            pltpu.VMEM((HALF, 2, WIDTH), BF16),
            pltpu.VMEM((HALF, HALF), F32),
            pltpu.VMEM((1, HALF), jnp.int32),
            pltpu.VMEM((N_TILE, 1, HALF), jnp.int32),
            pltpu.VMEM((N_TILE * 16, HALF), F32),
            pltpu.VMEM((2, N_TILE) + unit, BF16),
            pltpu.VMEM((2, N_TILE) + unit, BF16),
            pltpu.VMEM(pair, BF16),
            pltpu.VMEM(turned, BF16),
            pltpu.VMEM(pair, BF16),
            pltpu.VMEM((WIDTH, ROWS), BF16),
            pltpu.VMEM(pair, BF16),
            pltpu.VMEM(turned, BF16),
            pltpu.VMEM(pair, BF16),
            pltpu.VMEM((WIDTH, ROWS), BF16),
            pltpu.VMEM(turned, BF16),
            pltpu.VMEM((2, HEADS // GROUP, 2, HALF, GROUP * HALF), BF16),
            pltpu.VMEM((ROWS, WIDTH), BF16),
            pltpu.VMEM((WIDTH, ROWS), BF16),
            pltpu.VMEM((2, 3, ROWS, WIDTH), BF16),
            pltpu.VMEM((ROWS, WIDTH), F32),
            pltpu.VMEM((2, 2, 2, 4, N_Y, N_Z) + unit, BF16),
            pltpu.VMEM((2, 2, 4, N_Y, N_Z) + unit, BF16),
            pltpu.VMEM((2, N_X, N_Y, N_Z) + unit, BF16),
            pltpu.VMEM((2, N_Y, N_X, N_Z) + unit, BF16),
            pltpu.VMEM((2, N_X - 1, N_Y, N_Z) + unit, BF16),
            pltpu.VMEM((2, N_Y - 1, N_X, N_Z) + unit, BF16),
            pltpu.VMEM((2, N_Y, N_Z) + unit, BF16),
            pltpu.VMEM((2, N_X, N_Z) + unit, BF16),
            pltpu.VMEM((2, N_Y - 1, N_Z) + unit, BF16),
            pltpu.VMEM((2, N_X - 1, N_Z) + unit, BF16),
            pltpu.VMEM((2, N_Z, 2) + unit, BF16),
            pltpu.VMEM((2, N_Z - 1, 2) + unit, BF16),
            pltpu.SemaphoreType.DMA((7,)),
            pltpu.SemaphoreType.DMA((3,)),
            pltpu.SemaphoreType.DMA((N_SEM,)),
            pltpu.SemaphoreType.DMA((N_SEM,)),
        ],
        compiler_params=pltpu.CompilerParams(
            collective_id=0, has_side_effects=True, vmem_limit_bytes=62 * 1024 * 1024
        ),
    )(
        block_position,
        block_frame,
        block_count,
        blocks.reshape(ROWS, WIDTH),
        weights,
        cotangent.reshape(HALF, 2, WIDTH),
    )
    mixed, input_grad, weight_grad = pl.pallas_call(
        hand_over,
        out_shape=out_shape,
        in_specs=[hbm] * 3,
        out_specs=(hbm, hbm, hbm),
        scratch_shapes=[pltpu.VMEM(leaf.shape, leaf.dtype) for leaf in out_shape]
        + [pltpu.SemaphoreType.DMA((3,))] * 2,
        compiler_params=pltpu.CompilerParams(vmem_limit_bytes=62 * 1024 * 1024),
        name="hand_over",
    )(*results)
    return mixed.reshape(cotangent.shape), input_grad.reshape(blocks.shape), weight_grad


def solution(mesh):
    return jax.shard_map(
        body,
        mesh=mesh,
        in_specs=(
            P("scene", "tile", None, None),
            P("scene", "tile"),
            P("scene", "tile"),
            P("scene", "tile"),
            P(),
            P("scene", None, None, "tile", None),
        ),
        out_specs=(
            P("scene", None, None, "tile", None),
            P("scene", "tile", None, None),
            P(None, ("scene", "tile"), None),
        ),
        check_vma=False,
    )
```

time: 82 us -> 68.5 us (0.84)
  local copies, waits for them, and re-layouts: 7.61 us -> 0 us
  Pallas kernels: 72.9 us -> 66.9 us
    pallas_call x1 -> x2, Pallas kernels: 72.9 us -> 66.9 us  [the longest x1 65.1 us: body(): pl.pallas_call(kernel, out_shape=out_shape, in_specs=[hbm] * 6, out_specs...]
    unnamed x10 -> x0, local copies, waits for them, and re-layouts: 5.76 us -> none
    reshape x2 -> x0, local copies, waits for them, and re-layouts: 1.86 us -> none  [the longest x1 1.05 us: body(): cotangent.reshape(ROWS, WIDTH)]
where the time goes in v2:
time: 68.5 us; the launch traced here: 68.2 us
  Pallas kernels  66.9 us (98%)
  between operations  1.29 us (2%)
    pallas_call x1, Pallas kernels, body(): pl.pallas_call(kernel, out_shape=out_shape, in_specs=[hbm] * 6, out_specs...  65.1 us
    pallas_call x1, Pallas kernels, body(): pl.pallas_call(hand_over, out_shape=out_shape, in_specs=[hbm] * 3, out_sp...  1.79 us

profile of v2, /device:TPU:32, one launch (start us, length us, event | category | flops | bytes accessed | tf_op | source)
XLA Modules:
  0.0 68.2 jit_solution(13960570408119829894)
XLA Ops:
  1.3 65.1 %shard_map.85 = (bf16[128,2,512]{2,1,0:T(2,128)(2,1)}, bf16[256,512]{1,0:T(8,128)(2,1)}, f32[2,8,512]{2,1,0:T(8,128)}) custom-call(s32[1,2]{1,0:T(1,128)} %position_in.1, s32[1,2]{1,0:T(1,128)} %frame_in.1, s32[1,1]{1,0:T(1,128)S(6)} %copy.9.count_in, bf16[256,512]{1,0:T(8,128)(2,1)} %bitcast.4, bf16[8,512,512]{2,1,0:T(8,128)(2,1)} %weights_in.1, ...), custom_call_target="tpu_custom_call" | custom-call | tf_op jit(solution)/shard_map/pallas_call | solution.py:495
  66.4 1.8 %hand_over.1 = (bf16[128,2,512]{2,1,0:T(2,128)(2,1)}, bf16[256,512]{1,0:T(8,128)(2,1)}, f32[2,8,512]{2,1,0:T(8,128)}) custom-call(bf16[128,2,512]{2,1,0:T(2,128)(2,1)} %get-tuple-element.9.refs_0_, bf16[256,512]{1,0:T(8,128)(2,1)} %get-tuple-element.10.refs_1_, f32[2,8,512]{2,1,0:T(8,128)} %get-tuple-element.11.refs_2_), custom_call_target="tpu_custom_call" | custom-call | tf_op jit(solution)/shard_map/hand_over/pallas_call | solution.py:559

commit v3 on v2

--- a/solution.py
+++ b/solution.py
@@ -18,8 +18,10 @@
 BF16, F32 = jnp.bfloat16, jnp.float32
 EXP2_SCALE = HEAD_DIM ** (-0.5) * 1.4426950408889634
 SCALE = HEAD_DIM ** (-0.5)
-TAGS, STATES, GRADS, CORE, FIRST_X, FIRST_Y, SECOND_Y, SECOND_X, LAST = 0, 1, 2, 3, 11, 13, 15, 17, 19
-N_SEM = 21
+TAGS, STATES, GRADS, CORE, FIRST, SECOND, LAST = 0, 1, 2, 3, 11, 19, 27
+N_SEM = 29
+N_GROUP = HEADS // GROUP
+N_PAIR = N_Z // 2
 
 
 def dot(left, right):
@@ -88,14 +90,10 @@
     grid,
     parts,
     got_core,
-    sum_a,
-    sum_b,
-    got_a,
-    got_b,
-    sum_a2,
-    sum_b2,
-    got_a2,
-    got_b2,
+    sum_one,
+    got_one,
+    sum_two,
+    got_two,
     last,
     got_last,
     in_sem,
@@ -184,9 +182,8 @@
         return jnp.concatenate([one_head(rows, h, axis) for h in range(GROUP)], axis=1 - axis)
 
     def attend(piece):
-        @pl.loop(0, HEADS // GROUP)
-        def _(g):
-            feats = pl.ds(pl.multiple_of(g * HALF, HALF), HALF)
+        for g in range(N_GROUP):
+            feats = slice(g * HALF, (g + 1) * HALF)
             for b in range(2):
                 own = slice(b * HALF, (b + 1) * HALF)
                 queries = query_t[feats, own]
@@ -200,13 +197,12 @@
                     share = 1.0 / jnp.sum(powers, axis=0, keepdims=True)
                     soft = (powers * share).astype(BF16)
                     soft_t[piece, g, b, :, h * HALF : (h + 1) * HALF] = soft
-                    head = pl.ds(pl.multiple_of(g * HALF + h * HEAD_DIM, HEAD_DIM), HEAD_DIM)
+                    head = slice(g * HALF + h * HEAD_DIM, g * HALF + (h + 1) * HEAD_DIM)
                     context_t[piece, head, own] = dot(value_t[head, own], soft).astype(BF16)
 
     def attend_back(piece, lower, upper):
-        @pl.loop(lower, upper)
-        def _(g):
-            feats = pl.ds(pl.multiple_of(g * HALF, HALF), HALF)
+        for g in range(lower, upper):
+            feats = slice(g * HALF, (g + 1) * HALF)
             for b in range(2):
                 own = slice(b * HALF, (b + 1) * HALF)
                 grads_t = grad_context_t[feats, own]
@@ -218,7 +214,7 @@
                     grad_soft = dot(values, one_head(grads_t, h, 0))
                     mean = jnp.sum(wide * grad_soft, axis=0, keepdims=True)
                     grad_scores.append((wide * (grad_soft - mean)).astype(BF16))
-                    head = pl.ds(pl.multiple_of(g * HALF + h * HEAD_DIM, HEAD_DIM), HEAD_DIM)
+                    head = slice(g * HALF + h * HEAD_DIM, g * HALF + (h + 1) * HEAD_DIM)
                     grad_queries.append(dot(key_t[piece, head, own], grad_scores[h]))
                 grad_queries = jnp.concatenate(grad_queries, axis=0)
                 grad_n[piece, 0, own, feats] = (grad_queries * SCALE).T.astype(BF16)
@@ -246,56 +242,25 @@
         along = jnp.mean(scaled * grad_normed, axis=-1, keepdims=True)
         return rest.astype(F32) + inverse * (grad_normed - scaled * along)
 
-    def put_part(piece, w, s, product):
-        split = product.reshape(N_Y * N_Z, 2, 8, 2 * HALF)
+    def put_part(piece, g, w, product):
+        split = product.reshape(N_Y * N_Z, 2, 8, HALF)
         for c in range(2):
-            unit = jnp.concatenate([split[:, c, :, :HALF], split[:, c, :, HALF:]], axis=1)
-            parts[piece, c, s, w] = unit.astype(BF16).reshape(N_Y, N_Z, 16, HALF)
-
-    def core_parts(s, output):
-        return (s, 3) if output else (s, pl.ds(0, 3))
-
-    def core_sem(piece, s, output):
-        return CORE + 4 * piece + 2 * s + output
-
-    def send_core(piece, s, output):
-        at = core_parts(s, output)
-        start(
-            parts.at[(piece, 1 - core) + at],
-            got_core.at[(piece,) + at],
-            core_sem(piece, s, output),
-            peer_core,
-        )
+            parts[piece, c, g, w] = (
+                split[:, c].reshape(N_Y, N_PAIR, 16, HALF).astype(BF16)
+            )
 
     def context_sum(piece, rest):
-        for s in range(2):
-            put_part(piece, 3, s, dot(context_t[piece], rest[:, 2 * HALF * s : 2 * HALF * (s + 1)]))
-            send_core(piece, s, 1)
-
-    def normed_sum(piece, s):
-        chunk = slice(2 * HALF * s, 2 * HALF * (s + 1))
+        product = dot(context_t[piece], rest)
+        for g in range(N_GROUP):
+            put_part(piece, g, 3, product[:, g * HALF : (g + 1) * HALF])
+
+    def normed_sum(piece, g):
+        chunk = slice(g * HALF, (g + 1) * HALF)
+        grads = jnp.concatenate([grad_n[piece, w, :, chunk] for w in range(3)], axis=1)
+        product = dot(normed_t[piece], grads)
         for w in range(3):
-            put_part(piece, w, s, dot(normed_t[piece], grad_n[piece, w, :, chunk]))
-        send_core(piece, s, 0)
-
-    def sum_core(piece, s):
-        for output in (1, 0):
-            wait(recv_sem, got_core.at[(piece,) + core_parts(s, output)], core_sem(piece, s, output))
-        for w in range(4):
-            for j in range(N_Y):
-                total = (
-                    parts[piece, core, s, w, j].astype(F32) + got_core[piece, s, w, j].astype(F32)
-                ).astype(BF16)
-                if s == 0:
-                    sum_a[piece, w, j] = total
-                else:
-                    sum_b[piece, j, w] = total
-        if s == 0:
-            for d in range(1, N_X):
-                start(sum_a.at[piece, lax.rem(x + d, N_X)], got_a.at[piece, d - 1], FIRST_X + piece, peers_x[d - 1])
-        else:
-            for d in range(1, N_Y):
-                start(sum_b.at[piece, lax.rem(y + d, N_Y)], got_b.at[piece, d - 1], FIRST_Y + piece, peers_y[d - 1])
+            put_part(piece, g, w, product[:, w * HALF : (w + 1) * HALF])
+        start(parts.at[piece, 1 - core, g], got_core.at[piece, g], CORE + 4 * piece + g, peer_core)
 
     def add_up(own, got, n):
         total = own.astype(F32)
@@ -303,23 +268,37 @@
             total += got[d].astype(F32)
         return total
 
-    def sum_first(piece, s):
-        if s == 0:
-            wait(recv_sem, got_a.at[piece], FIRST_X + piece)
-            sum_a2[piece] = add_up(sum_a[piece, x], [got_a[piece, d] for d in range(N_X - 1)], N_X).astype(BF16)
-            for d in range(1, N_Y):
-                start(sum_a2.at[piece, lax.rem(y + d, N_Y)], got_a2.at[piece, d - 1], SECOND_Y + piece, peers_y[d - 1])
-        else:
-            wait(recv_sem, got_b.at[piece], FIRST_Y + piece)
-            sum_b2[piece] = add_up(sum_b[piece, y], [got_b[piece, d] for d in range(N_Y - 1)], N_Y).astype(BF16)
-            for d in range(1, N_X):
-                start(sum_b2.at[piece, lax.rem(x + d, N_X)], got_b2.at[piece, d - 1], SECOND_X + piece, peers_x[d - 1])
+    def send_one(piece, g):
+        me, peers = (x, peers_x) if g % 2 == 0 else (y, peers_y)
+        for d in range(1, 4):
+            start(sum_one.at[piece, g, lax.rem(me + d, 4)], got_one.at[piece, g, d - 1], FIRST + 4 * piece + g, peers[d - 1])
+
+    def sum_core(piece, g):
+        wait(recv_sem, got_core.at[piece, g], CORE + 4 * piece + g)
+        for w in range(4):
+            for j in range(N_Y):
+                at = (w, j) if g % 2 == 0 else (j, w)
+                sum_one[(piece, g) + at] = (
+                    parts[piece, core, g, w, j].astype(F32) + got_core[piece, g, w, j].astype(F32)
+                ).astype(BF16)
+        send_one(piece, g)
+
+    def sum_first(piece, g):
+        first, second, peers = (x, y, peers_y) if g % 2 == 0 else (y, x, peers_x)
+        wait(recv_sem, got_one.at[piece, g], FIRST + 4 * piece + g)
+        sum_two[piece, g] = add_up(sum_one[piece, g, first], [got_one[piece, g, d] for d in range(3)], 4).astype(BF16)
+        for d in range(1, 4):
+            start(sum_two.at[piece, g, lax.rem(second + d, 4)], got_two.at[piece, g, d - 1], SECOND + 4 * piece + g, peers[d - 1])
 
     def sum_second(piece):
-        wait(recv_sem, got_a2.at[piece], SECOND_Y + piece)
-        last[piece, :, 0] = add_up(sum_a2[piece, y], [got_a2[piece, d] for d in range(N_Y - 1)], N_Y).astype(BF16)
-        wait(recv_sem, got_b2.at[piece], SECOND_X + piece)
-        last[piece, :, 1] = add_up(sum_b2[piece, x], [got_b2[piece, d] for d in range(N_X - 1)], N_X).astype(BF16)
+        for s in range(2):
+            halves = []
+            for g in (2 * s, 2 * s + 1):
+                second = y if g % 2 == 0 else x
+                wait(recv_sem, got_two.at[piece, g], SECOND + 4 * piece + g)
+                total = add_up(sum_two[piece, g, second], [got_two[piece, g, d] for d in range(3)], 4)
+                halves.append(total.reshape(N_Z, 8, HALF))
+            last[piece, :, s] = jnp.concatenate(halves, axis=1).astype(BF16)
         for d in range(1, N_Z):
             start(last.at[piece, lax.rem(z + d, N_Z)], got_last.at[piece, d - 1], LAST + piece, peers_z[d - 1])
 
@@ -400,7 +379,7 @@
     project(TEMPORAL, grid[...])
     key_t[TEMPORAL] = key_n[TEMPORAL].T
     attend(TEMPORAL)
-    attend_back(TEMPORAL, 0, HEADS // GROUP)
+    attend_back(TEMPORAL, 0, N_GROUP)
     grid_grad = input_back(TEMPORAL, grid[...], rest).astype(BF16)
     for j in range(2):
         back = dot(placing, grid_grad[j * HALF : (j + 1) * HALF])
@@ -415,14 +394,14 @@
 
     context_sum(TEMPORAL, rest)
     normed_t[TEMPORAL] = normed_n[TEMPORAL].T
-    normed_sum(TEMPORAL, 0)
-    normed_sum(TEMPORAL, 1)
+    for g in range(N_GROUP):
+        normed_sum(TEMPORAL, g)
     temporal = grid[...] + dot_tn(context_t[TEMPORAL], weights[7])
     for j in range(2):
         mixed_out[:, j, :] = jnp.where(active_wide, temporal[j * HALF : (j + 1) * HALF], 0.0).astype(BF16)
     stores[0].start()
-    sum_core(TEMPORAL, 0)
-    sum_core(TEMPORAL, 1)
+    for g in range(N_GROUP):
+        sum_core(TEMPORAL, g)
 
     wait(recv_sem, box_in.at[1, pl.ds(0, N_TILE - 1)], GRADS)
     spread[...] = box_in[1].reshape(N_TILE * 16, HALF).astype(F32)
@@ -435,19 +414,21 @@
     ).astype(BF16)
     context_sum(SPATIAL, rest)
     context_back(SPATIAL, rest)
-    attend_back(SPATIAL, 0, 2)
-    normed_sum(SPATIAL, 0)
-    sum_first(TEMPORAL, 0)
-    sum_first(TEMPORAL, 1)
-    attend_back(SPATIAL, 2, 4)
-    normed_sum(SPATIAL, 1)
-    sum_core(SPATIAL, 0)
+    for g in range(N_GROUP):
+        attend_back(SPATIAL, g, g + 1)
+        normed_sum(SPATIAL, g)
+        if g > 0:
+            sum_core(SPATIAL, g - 1)
+        if g == 1:
+            for group in range(N_GROUP):
+                sum_first(TEMPORAL, group)
+    input_grad = input_back(SPATIAL, blocks[...].astype(F32), rest).astype(BF16)
+    sum_core(SPATIAL, N_GROUP - 1)
+    grad_out[...] = input_grad
+    stores[1].start()
     sum_second(TEMPORAL)
-    sum_core(SPATIAL, 1)
-    grad_out[...] = input_back(SPATIAL, blocks[...].astype(F32), rest).astype(BF16)
-    stores[1].start()
-    sum_first(SPATIAL, 0)
-    sum_first(SPATIAL, 1)
+    for g in range(N_GROUP):
+        sum_first(SPATIAL, g)
     sum_last(TEMPORAL)
     sum_second(SPATIAL)
     sum_last(SPATIAL)
@@ -457,13 +438,10 @@
     wait(send_sem, box_in.at[0, pl.ds(0, N_TILE - 1)], STATES)
     wait(send_sem, box_in.at[1, pl.ds(0, N_TILE - 1)], GRADS)
     for piece in range(2):
-        for s in range(2):
-            for output in range(2):
-                wait(send_sem, got_core.at[(piece,) + core_parts(s, output)], core_sem(piece, s, output))
-        wait(send_sem, got_a.at[piece], FIRST_X + piece)
-        wait(send_sem, got_b.at[piece], FIRST_Y + piece)
-        wait(send_sem, got_a2.at[piece], SECOND_Y + piece)
-        wait(send_sem, got_b2.at[piece], SECOND_X + piece)
+        for g in range(N_GROUP):
+            wait(send_sem, got_core.at[piece, g], CORE + 4 * piece + g)
+            wait(send_sem, got_one.at[piece, g], FIRST + 4 * piece + g)
+            wait(send_sem, got_two.at[piece, g], SECOND + 4 * piece + g)
         wait(send_sem, got_last.at[piece], LAST + piece)
     for store in stores:
         store.wait()
@@ -523,21 +501,17 @@
             pltpu.VMEM(pair, BF16),
             pltpu.VMEM((WIDTH, ROWS), BF16),
             pltpu.VMEM(turned, BF16),
-            pltpu.VMEM((2, HEADS // GROUP, 2, HALF, GROUP * HALF), BF16),
+            pltpu.VMEM((2, N_GROUP, 2, HALF, GROUP * HALF), BF16),
             pltpu.VMEM((ROWS, WIDTH), BF16),
             pltpu.VMEM((WIDTH, ROWS), BF16),
             pltpu.VMEM((2, 3, ROWS, WIDTH), BF16),
             pltpu.VMEM((ROWS, WIDTH), F32),
-            pltpu.VMEM((2, 2, 2, 4, N_Y, N_Z) + unit, BF16),
-            pltpu.VMEM((2, 2, 4, N_Y, N_Z) + unit, BF16),
-            pltpu.VMEM((2, N_X, N_Y, N_Z) + unit, BF16),
-            pltpu.VMEM((2, N_Y, N_X, N_Z) + unit, BF16),
-            pltpu.VMEM((2, N_X - 1, N_Y, N_Z) + unit, BF16),
-            pltpu.VMEM((2, N_Y - 1, N_X, N_Z) + unit, BF16),
-            pltpu.VMEM((2, N_Y, N_Z) + unit, BF16),
-            pltpu.VMEM((2, N_X, N_Z) + unit, BF16),
-            pltpu.VMEM((2, N_Y - 1, N_Z) + unit, BF16),
-            pltpu.VMEM((2, N_X - 1, N_Z) + unit, BF16),
+            pltpu.VMEM((2, 2, N_GROUP, 4, N_Y, N_PAIR) + unit, BF16),
+            pltpu.VMEM((2, N_GROUP, 4, N_Y, N_PAIR) + unit, BF16),
+            pltpu.VMEM((2, N_GROUP, 4, 4, N_PAIR) + unit, BF16),
+            pltpu.VMEM((2, N_GROUP, 3, 4, N_PAIR) + unit, BF16),
+            pltpu.VMEM((2, N_GROUP, 4, N_PAIR) + unit, BF16),
+            pltpu.VMEM((2, N_GROUP, 3, N_PAIR) + unit, BF16),
             pltpu.VMEM((2, N_Z, 2) + unit, BF16),
             pltpu.VMEM((2, N_Z - 1, 2) + unit, BF16),
             pltpu.SemaphoreType.DMA((7,)),

time: 68.5 us -> 62.6 us (0.914)
  Pallas kernels: 66.9 us -> 61 us
    pallas_call x1, Pallas kernels: 65.1 us -> 59.2 us  [body(): pl.pallas_call(kernel, out_shape=out_shape, in_specs=[hbm] * 6, out_specs...]
where the time goes in v3:
time: 62.6 us; the launch traced here: 62.5 us
  Pallas kernels  61 us (97%)
  between operations  1.45 us (2%)
    pallas_call x1, Pallas kernels, body(): pl.pallas_call(kernel, out_shape=out_shape, in_specs=[hbm] * 6, out_specs...  59.2 us
    pallas_call x1, Pallas kernels, body(): pl.pallas_call(hand_over, out_shape=out_shape, in_specs=[hbm] * 3, out_sp...  1.79 us

profile of v3, /device:TPU:32, one launch (start us, length us, event | category | flops | bytes accessed | tf_op | source)
XLA Modules:
  0.0 62.5 jit_solution(579324838221519268)
XLA Ops:
  1.3 59.2 %shard_map.85 = (bf16[128,2,512]{2,1,0:T(2,128)(2,1)}, bf16[256,512]{1,0:T(8,128)(2,1)}, f32[2,8,512]{2,1,0:T(8,128)}) custom-call(s32[1,2]{1,0:T(1,128)} %position_in.1, s32[1,2]{1,0:T(1,128)} %frame_in.1, s32[1,1]{1,0:T(1,128)S(6)} %copy.9.count_in, bf16[256,512]{1,0:T(8,128)(2,1)} %bitcast.4, bf16[8,512,512]{2,1,0:T(8,128)(2,1)} %weights_in.1, ...), custom_call_target="tpu_custom_call" | custom-call | tf_op jit(solution)/shard_map/pallas_call | solution.py:473
  60.5 1.8 %hand_over.1 = (bf16[128,2,512]{2,1,0:T(2,128)(2,1)}, bf16[256,512]{1,0:T(8,128)(2,1)}, f32[2,8,512]{2,1,0:T(8,128)}) custom-call(bf16[128,2,512]{2,1,0:T(2,128)(2,1)} %get-tuple-element.9.refs_0_, bf16[256,512]{1,0:T(8,128)(2,1)} %get-tuple-element.10.refs_1_, f32[2,8,512]{2,1,0:T(8,128)} %get-tuple-element.11.refs_2_), custom_call_target="tpu_custom_call" | custom-call | tf_op jit(solution)/shard_map/hand_over/pallas_call | solution.py:533

commit v4 on v3

--- a/solution.py
+++ b/solution.py
@@ -18,8 +18,8 @@
 BF16, F32 = jnp.bfloat16, jnp.float32
 EXP2_SCALE = HEAD_DIM ** (-0.5) * 1.4426950408889634
 SCALE = HEAD_DIM ** (-0.5)
-TAGS, STATES, GRADS, CORE, FIRST, SECOND, LAST = 0, 1, 2, 3, 11, 19, 27
-N_SEM = 29
+TAGS, STATES, GRADS, CORE, FIRST, SECOND, LAST = 0, 1, 3, 5, 13, 21, 29
+N_SEM = 31
 N_GROUP = HEADS // GROUP
 N_PAIR = N_Z // 2
 
@@ -134,8 +134,7 @@
 
     barrier = pltpu.get_barrier_semaphore()
 
-    @pl.loop(1, N_TILE)
-    def _(d):
+    for d in range(1, N_TILE):
         pl.semaphore_signal(
             barrier, inc=1, device_id=(x, lax.rem(t + d, N_TILE)), device_id_type=MESH
         )
@@ -162,17 +161,17 @@
             to = lax.rem(t + d, N_TILE)
             start(outgoing(to), incoming.at[t], sem, (x, to))
 
-    def project(piece, rows):
+    def project(piece, rows, own):
         scaled = (rows * inverse_norm(rows)).astype(BF16)
-        normed_n[piece] = scaled
+        normed_n[piece, own] = scaled
         first = 4 * piece
         queries = dot(scaled, weights[first]).astype(BF16)
-        query_n[piece] = queries
-        query_t[...] = queries.T
-        key_n[piece] = dot(scaled, weights[first + 1]).astype(BF16)
+        query_n[piece, own] = queries
+        query_t[:, own] = queries.T
+        key_n[piece, own] = dot(scaled, weights[first + 1]).astype(BF16)
         values = dot(scaled, weights[first + 2]).astype(BF16)
-        value_n[piece] = values
-        value_t[...] = values.T
+        value_n[piece, own] = values
+        value_t[:, own] = values.T
 
     def one_head(rows, h, axis):
         owner = iota((HALF, HALF), axis) // HEAD_DIM
@@ -181,10 +180,10 @@
     def by_head(rows, axis):
         return jnp.concatenate([one_head(rows, h, axis) for h in range(GROUP)], axis=1 - axis)
 
-    def attend(piece):
-        for g in range(N_GROUP):
+    def attend(piece, lower, upper, halves):
+        for g in range(lower, upper):
             feats = slice(g * HALF, (g + 1) * HALF)
-            for b in range(2):
+            for b in halves:
                 own = slice(b * HALF, (b + 1) * HALF)
                 queries = query_t[feats, own]
                 keys = key_n[piece, own, feats]
@@ -200,10 +199,10 @@
                     head = slice(g * HALF + h * HEAD_DIM, g * HALF + (h + 1) * HEAD_DIM)
                     context_t[piece, head, own] = dot(value_t[head, own], soft).astype(BF16)
 
-    def attend_back(piece, lower, upper):
+    def attend_back(piece, lower, upper, halves):
         for g in range(lower, upper):
             feats = slice(g * HALF, (g + 1) * HALF)
-            for b in range(2):
+            for b in halves:
                 own = slice(b * HALF, (b + 1) * HALF)
                 grads_t = grad_context_t[feats, own]
                 values = value_n[piece, own, feats]
@@ -230,13 +229,15 @@
         grad_context_n[...] = grads
         grad_context_t[...] = grads.T
 
-    def input_back(piece, rows, rest):
+    def normed_back(piece, own):
         first = 4 * piece
-        grad_normed = (
-            dot(grad_n[piece, 0], weights_t[first])
-            + dot(grad_n[piece, 1], weights_t[first + 1])
-            + dot(grad_n[piece, 2], weights_t[first + 2])
+        return (
+            dot(grad_n[piece, 0, own], weights_t[first])
+            + dot(grad_n[piece, 1, own], weights_t[first + 1])
+            + dot(grad_n[piece, 2, own], weights_t[first + 2])
         )
+
+    def input_back(rows, rest, grad_normed):
         inverse = inverse_norm(rows)
         scaled = rows * inverse
         along = jnp.mean(scaled * grad_normed, axis=-1, keepdims=True)
@@ -313,8 +314,10 @@
 
     loads[0].wait()
     loads[1].wait()
-    project(SPATIAL, blocks[...].astype(F32))
-
+    whole, both = slice(0, ROWS), (0, 1)
+    project(SPATIAL, blocks[...].astype(F32), whole)
+
+    attend(SPATIAL, 0, 3, both)
     lane = iota((1, HALF), 1)
     for i in range(2, 5):
         loads[i].wait()
@@ -325,7 +328,7 @@
     pl.semaphore_wait(barrier, N_TILE - 1 + N_X - 1)
     send_all(lambda to: tag_out, tag_in, TAGS)
 
-    attend(SPATIAL)
+    attend(SPATIAL, 3, 4, both)
     loads[5].wait()
     states = blocks[...].astype(F32) + dot_tn(context_t[SPATIAL], weights[3])
     for s in range(2):
@@ -333,9 +336,10 @@
             spread[pl.ds(4 * s + k, HALF, stride=8), :] = states[
                 s * HALF : (s + 1) * HALF, k * HALF : (k + 1) * HALF
             ]
-    box_out[0] = spread[...].astype(BF16).reshape(N_TILE, 16, HALF)
-    box_in[0, t] = box_out[0, t]
-    send_all(lambda to: box_out.at[0, to], box_in.at[0], STATES)
+    for j in range(2):
+        box_out[0, j] = spread[...].reshape(N_TILE, 2, 8, HALF)[:, j].astype(BF16)
+        box_in[0, j, t] = box_out[0, j, t]
+        send_all(lambda to: box_out.at[0, j, to], box_in.at[0, j], STATES + j)
 
     for w in range(8):
         weights_t[w] = weights[w].T
@@ -362,35 +366,35 @@
     ).astype(BF16)
     context_back(TEMPORAL, rest)
 
-    wait(recv_sem, box_in.at[0, pl.ds(0, N_TILE - 1)], STATES)
-    spread[...] = box_in[0].reshape(N_TILE * 16, HALF).astype(F32)
     for j in range(2):
+        own = slice(j * HALF, (j + 1) * HALF)
+        wait(recv_sem, box_in.at[0, j, pl.ds(0, N_TILE - 1)], STATES + j)
+        start_row = j * N_TILE * 8
+        spread[start_row : start_row + N_TILE * 8] = box_in[0, j].astype(F32).reshape(N_TILE * 8, HALF)
         rows = jnp.concatenate(
             [
                 jnp.concatenate(
-                    [spread[pl.ds(8 * j + 4 * s + k, N_TILE, stride=16), :] for k in range(4)], axis=1
+                    [spread[pl.ds(start_row + 4 * s + k, N_TILE, stride=8), :] for k in range(4)], axis=1
                 )
                 for s in range(2)
             ],
             axis=0,
         ).astype(BF16)
-        grid[j * HALF : (j + 1) * HALF] = dot_tn(placing, rows)
-
-    project(TEMPORAL, grid[...])
-    key_t[TEMPORAL] = key_n[TEMPORAL].T
-    attend(TEMPORAL)
-    attend_back(TEMPORAL, 0, N_GROUP)
-    grid_grad = input_back(TEMPORAL, grid[...], rest).astype(BF16)
-    for j in range(2):
-        back = dot(placing, grid_grad[j * HALF : (j + 1) * HALF])
+        grid[own] = dot_tn(placing, rows)
+        project(TEMPORAL, grid[own], own)
+        key_t[TEMPORAL, :, own] = key_n[TEMPORAL, own].T
+        attend(TEMPORAL, 0, N_GROUP, (j,))
+        attend_back(TEMPORAL, 0, N_GROUP, (j,))
+        grid_grad = input_back(grid[own], rest[own], normed_back(TEMPORAL, own)).astype(BF16)
+        back = dot(placing, grid_grad)
         for s in range(2):
             for k in range(4):
-                spread[pl.ds(8 * j + 4 * s + k, N_TILE, stride=16), :] = back[
+                spread[pl.ds(start_row + 4 * s + k, N_TILE, stride=8), :] = back[
                     s * N_TILE : (s + 1) * N_TILE, k * HALF : (k + 1) * HALF
                 ]
-    box_out[1] = spread[...].astype(BF16).reshape(N_TILE, 16, HALF)
-    box_in[1, t] = box_out[1, t]
-    send_all(lambda to: box_out.at[1, to], box_in.at[1], GRADS)
+        box_out[1, j] = spread[start_row : start_row + N_TILE * 8].reshape(N_TILE, 8, HALF).astype(BF16)
+        box_in[1, j, t] = box_out[1, j, t]
+        send_all(lambda to: box_out.at[1, j, to], box_in.at[1, j], GRADS + j)
 
     context_sum(TEMPORAL, rest)
     normed_t[TEMPORAL] = normed_n[TEMPORAL].T
@@ -403,8 +407,11 @@
     for g in range(N_GROUP):
         sum_core(TEMPORAL, g)
 
-    wait(recv_sem, box_in.at[1, pl.ds(0, N_TILE - 1)], GRADS)
-    spread[...] = box_in[1].reshape(N_TILE * 16, HALF).astype(F32)
+    for j in range(2):
+        wait(recv_sem, box_in.at[1, j, pl.ds(0, N_TILE - 1)], GRADS + j)
+    spread[...] = jnp.concatenate(
+        [box_in[1, j].astype(F32) for j in range(2)], axis=1
+    ).reshape(N_TILE * 16, HALF)
     rest = jnp.concatenate(
         [
             jnp.concatenate([spread[pl.ds(4 * s + k, HALF, stride=8), :] for k in range(4)], axis=1)
@@ -415,28 +422,31 @@
     context_sum(SPATIAL, rest)
     context_back(SPATIAL, rest)
     for g in range(N_GROUP):
-        attend_back(SPATIAL, g, g + 1)
+        attend_back(SPATIAL, g, g + 1, both)
         normed_sum(SPATIAL, g)
         if g > 0:
             sum_core(SPATIAL, g - 1)
         if g == 1:
             for group in range(N_GROUP):
                 sum_first(TEMPORAL, group)
-    input_grad = input_back(SPATIAL, blocks[...].astype(F32), rest).astype(BF16)
+    grad_normed = normed_back(SPATIAL, whole)
     sum_core(SPATIAL, N_GROUP - 1)
-    grad_out[...] = input_grad
+    grad_out[...] = input_back(blocks[...].astype(F32), rest, grad_normed).astype(BF16)
     stores[1].start()
+    sum_first(SPATIAL, 0)
+    sum_first(SPATIAL, 1)
     sum_second(TEMPORAL)
-    for g in range(N_GROUP):
-        sum_first(SPATIAL, g)
+    sum_first(SPATIAL, 2)
+    sum_first(SPATIAL, 3)
     sum_last(TEMPORAL)
     sum_second(SPATIAL)
     sum_last(SPATIAL)
     stores[2].start()
 
     wait(send_sem, tag_in.at[pl.ds(0, N_TILE - 1)], TAGS)
-    wait(send_sem, box_in.at[0, pl.ds(0, N_TILE - 1)], STATES)
-    wait(send_sem, box_in.at[1, pl.ds(0, N_TILE - 1)], GRADS)
+    for j in range(2):
+        wait(send_sem, box_in.at[0, j, pl.ds(0, N_TILE - 1)], STATES + j)
+        wait(send_sem, box_in.at[1, j, pl.ds(0, N_TILE - 1)], GRADS + j)
     for piece in range(2):
         for g in range(N_GROUP):
             wait(send_sem, got_core.at[piece, g], CORE + 4 * piece + g)
@@ -490,8 +500,8 @@
             pltpu.VMEM((1, HALF), jnp.int32),
             pltpu.VMEM((N_TILE, 1, HALF), jnp.int32),
             pltpu.VMEM((N_TILE * 16, HALF), F32),
-            pltpu.VMEM((2, N_TILE) + unit, BF16),
-            pltpu.VMEM((2, N_TILE) + unit, BF16),
+            pltpu.VMEM((2, 2, N_TILE, 8, HALF), BF16),
+            pltpu.VMEM((2, 2, N_TILE, 8, HALF), BF16),
             pltpu.VMEM(pair, BF16),
             pltpu.VMEM(turned, BF16),
             pltpu.VMEM(pair, BF16),

time: 62.6 us -> 60.6 us (0.968); the launches traced: 62.5 us -> 59.5 us
  Pallas kernels: 61 us -> 58 us
    pallas_call x1, Pallas kernels: 59.2 us -> 56.2 us  [body(): pl.pallas_call(kernel, out_shape=out_shape, in_specs=[hbm] * 6, out_specs...]
where the time goes in v4:
time: 60.6 us; the launch traced here: 59.5 us
  Pallas kernels  58 us (96%)
  between operations  1.45 us (2%)
    pallas_call x1, Pallas kernels, body(): pl.pallas_call(kernel, out_shape=out_shape, in_specs=[hbm] * 6, out_specs...  56.2 us
    pallas_call x1, Pallas kernels, body(): pl.pallas_call(hand_over, out_shape=out_shape, in_specs=[hbm] * 3, out_sp...  1.79 us

profile of v4, /device:TPU:32, one launch (start us, length us, event | category | flops | bytes accessed | tf_op | source)
XLA Modules:
  0.0 59.5 jit_solution(17009272315445734957)
XLA Ops:
  1.3 56.2 %shard_map.85 = (bf16[128,2,512]{2,1,0:T(2,128)(2,1)}, bf16[256,512]{1,0:T(8,128)(2,1)}, f32[2,8,512]{2,1,0:T(8,128)}) custom-call(s32[1,2]{1,0:T(1,128)} %position_in.1, s32[1,2]{1,0:T(1,128)} %frame_in.1, s32[1,1]{1,0:T(1,128)S(6)} %copy.9.count_in, bf16[256,512]{1,0:T(8,128)(2,1)} %bitcast.4, bf16[8,512,512]{2,1,0:T(8,128)(2,1)} %weights_in.1, ...), custom_call_target="tpu_custom_call" | custom-call | tf_op jit(solution)/shard_map/pallas_call | solution.py:483
  57.5 1.8 %hand_over.1 = (bf16[128,2,512]{2,1,0:T(2,128)(2,1)}, bf16[256,512]{1,0:T(8,128)(2,1)}, f32[2,8,512]{2,1,0:T(8,128)}) custom-call(bf16[128,2,512]{2,1,0:T(2,128)(2,1)} %get-tuple-element.9.refs_0_, bf16[256,512]{1,0:T(8,128)(2,1)} %get-tuple-element.10.refs_1_, f32[2,8,512]{2,1,0:T(8,128)} %get-tuple-element.11.refs_2_), custom_call_target="tpu_custom_call" | custom-call | tf_op jit(solution)/shard_map/hand_over/pallas_call | solution.py:543

commit v5 on v4

--- a/solution.py
+++ b/solution.py
@@ -423,10 +423,10 @@
     context_back(SPATIAL, rest)
     for g in range(N_GROUP):
         attend_back(SPATIAL, g, g + 1, both)
-        normed_sum(SPATIAL, g)
         if g > 0:
             sum_core(SPATIAL, g - 1)
-        if g == 1:
+        normed_sum(SPATIAL, g)
+        if g == 2:
             for group in range(N_GROUP):
                 sum_first(TEMPORAL, group)
     grad_normed = normed_back(SPATIAL, whole)
@@ -459,8 +459,9 @@
 
 def hand_over(*refs):
     sources, targets, held, sem_in, sem_out = refs[:3], refs[3:6], refs[6:9], refs[9], refs[10]
-    loads = [pltpu.make_async_copy(sources[i], held[i], sem_in.at[i]) for i in range(3)]
-    stores = [pltpu.make_async_copy(held[i], targets[i], sem_out.at[i]) for i in range(3)]
+    pieces = [(i, pl.ds(q * n, n)) for i, n in ((0, HALF // 4), (1, ROWS // 4)) for q in range(4)] + [(2, pl.ds(0, 2))]
+    loads = [pltpu.make_async_copy(sources[i].at[at], held[i].at[at], sem_in.at[q]) for q, (i, at) in enumerate(pieces)]
+    stores = [pltpu.make_async_copy(held[i].at[at], targets[i].at[at], sem_out.at[q]) for q, (i, at) in enumerate(pieces)]
     for load in loads:
         load.start()
     for load, store in zip(loads, stores):
@@ -546,7 +547,7 @@
         in_specs=[hbm] * 3,
         out_specs=(hbm, hbm, hbm),
         scratch_shapes=[pltpu.VMEM(leaf.shape, leaf.dtype) for leaf in out_shape]
-        + [pltpu.SemaphoreType.DMA((3,))] * 2,
+        + [pltpu.SemaphoreType.DMA((9,))] * 2,
         compiler_params=pltpu.CompilerParams(vmem_limit_bytes=62 * 1024 * 1024),
         name="hand_over",
     )(*results)

time: 60.6 us -> 59.9 us (0.988); the launches traced: 59.5 us -> 59.7 us
  no operation moved by 1% of the time
where the time goes in v5:
time: 59.9 us; the launch traced here: 59.7 us
  Pallas kernels  58.3 us (97%)
  between operations  1.45 us (2%)
    pallas_call x1, Pallas kernels, body(): pl.pallas_call(kernel, out_shape=out_shape, in_specs=[hbm] * 6, out_specs...  56.4 us
    pallas_call x1, Pallas kernels, body(): pl.pallas_call(hand_over, out_shape=out_shape, in_specs=[hbm] * 3, out_sp...  1.86 us

profile of v5, /device:TPU:32, one launch (start us, length us, event | category | flops | bytes accessed | tf_op | source)
XLA Modules:
  0.0 59.7 jit_solution(9387782553333614195)
XLA Ops:
  1.3 56.4 %shard_map.85 = (bf16[128,2,512]{2,1,0:T(2,128)(2,1)}, bf16[256,512]{1,0:T(8,128)(2,1)}, f32[2,8,512]{2,1,0:T(8,128)}) custom-call(s32[1,2]{1,0:T(1,128)} %position_in.1, s32[1,2]{1,0:T(1,128)} %frame_in.1, s32[1,1]{1,0:T(1,128)S(6)} %copy.9.count_in, bf16[256,512]{1,0:T(8,128)(2,1)} %bitcast.4, bf16[8,512,512]{2,1,0:T(8,128)(2,1)} %weights_in.1, ...), custom_call_target="tpu_custom_call" | custom-call | tf_op jit(solution)/shard_map/pallas_call | solution.py:484
  57.7 1.9 %hand_over.1 = (bf16[128,2,512]{2,1,0:T(2,128)(2,1)}, bf16[256,512]{1,0:T(8,128)(2,1)}, f32[2,8,512]{2,1,0:T(8,128)}) custom-call(bf16[128,2,512]{2,1,0:T(2,128)(2,1)} %get-tuple-element.9.refs_0_, bf16[256,512]{1,0:T(8,128)(2,1)} %get-tuple-element.10.refs_1_, f32[2,8,512]{2,1,0:T(8,128)} %get-tuple-element.11.refs_2_), custom_call_target="tpu_custom_call" | custom-call | tf_op jit(solution)/shard_map/hand_over/pallas_call | solution.py:544
